TPU v7x, 32 devices: a whole 2x2x4 slice. The times are simulated.
32 devices in a mesh: dp: 32 (over z, y, x, core).
Axes of the slice: x: 2, y: 2, z: 4, core: 2. Of those that a mesh axis runs over, the one named last changes fastest.
Arguments:
- images: bfloat16 [256, 197, 512], P('dp'), may hold values from -6 to 6
- image_count: int32 [32], P('dp'), may hold values from 1 to 8, as said below
- expert_index: int32 [256, 197, 2], P('dp'), may hold values from 0 to 7, as said below
- expert_slot: int32 [256, 197, 2], P('dp'), may hold values from 0 to 127, as said below
- keep: int32 [256, 197, 2], P('dp'), may hold values from 0 to 1, as said below
- cotangent: bfloat16 [256, 197, 512], P('dp'), may hold values from -6 to 6
- ln1_gain: bfloat16 [512], P('dp'), may hold values from 0.5 to 1.5
- ln1_bias: bfloat16 [512], P('dp'), may hold values from -1.1953125 to 1.1953125
- qkv_weight: bfloat16 [512, 1536], P('dp'), may hold values from -0.375 to 0.375
- qv_bias: bfloat16 [2, 512], P(None, 'dp'), may hold values from -1.796875 to 1.796875
- out_weight: bfloat16 [512, 512], P('dp'), may hold values from -0.75 to 0.75
- out_bias: bfloat16 [512], P('dp'), may hold values from -0.59765625 to 0.59765625
- ln2_gain: bfloat16 [512], P('dp'), may hold values from 0.5 to 1.5
- ln2_bias: bfloat16 [512], P('dp'), may hold values from -0.59765625 to 0.59765625
- router_weight: bfloat16 [512, 8], P('dp'), may hold values from -0.1875 to 0.1875
- expert_in: bfloat16 [8, 512, 2048], P(None, 'dp'), may hold values from -0.25 to 0.25
- expert_in_bias: bfloat16 [8, 2048], P(None, 'dp'), may hold values from -1.1953125 to 1.1953125
- expert_out: bfloat16 [8, 2048, 512], P(None, 'dp'), may hold values from -0.75 to 0.75
- expert_out_bias: bfloat16 [8, 512], P(None, 'dp'), may hold values from -2.3 to 2.3
Outputs:
- block_out: bfloat16 [256, 197, 512], P('dp')
- image_grad: bfloat16 [256, 197, 512], P('dp')
- balance: float32 [], replicated
- ln1_gain_grad: float32 [512], P('dp')
- ln1_bias_grad: float32 [512], P('dp')
- qkv_weight_grad: float32 [512, 1536], P('dp')
- qv_bias_grad: float32 [2, 512], P(None, 'dp')
- out_weight_grad: float32 [512, 512], P('dp')
- out_bias_grad: float32 [512], P('dp')
- ln2_gain_grad: float32 [512], P('dp')
- ln2_bias_grad: float32 [512], P('dp')
- router_weight_grad: float32 [512, 8], P('dp')
- expert_in_grad: float32 [8, 512, 2048], P(None, 'dp')
- expert_in_bias_grad: float32 [8, 2048], P(None, 'dp')
- expert_out_grad: float32 [8, 2048, 512], P(None, 'dp')
- expert_out_bias_grad: float32 [8, 512], P(None, 'dp')
Inputs may be any that keep to these rules, and one draw needn't show every extreme that they name: Device d's live images fill its first image_count[d] slots; some device has all 8 slots live. `expert_index`: the two experts of a token differ. `expert_slot`: within one micro-batch of one device, the dispatched choices of one expert have distinct positions; choices that are not dispatched hold 0. In some micro-batch some expert uses all 128 positions. `keep`: choices of tokens in padding slots are never dispatched.
All inputs are finite; a program needn't handle non-finite values.
Results may differ from a plain program's by a relative error of at most 0.014.
Values may be sent and summed in bfloat16 or wider, within the bound.
No kernel may reach another device: no remote copies, remote signals or barrier semaphores. Data moves between devices by JAX's collectives and lax.ppermute only.
A program may use at most 384 MiB of HBM per device.

v0:
```python
import functools
import math

import jax
import jax.numpy as jnp
from jax import lax
from jax.experimental import pallas as pl
from jax.experimental.pallas import tpu as pltpu
from jax.sharding import PartitionSpec as P

HEADS = 8
HEAD_DIM = 64
EXPERTS = 8
MICRO = 4
CAP = 128
CHUNKS = (2, 2)
PAIR = 2 * HEAD_DIM
DISPATCH = 8

EPSILON = 1e-06
BALANCE_WEIGHT = 8.0

BF = jnp.bfloat16
F32 = jnp.float32

ROW_GAIN1, ROW_BIAS1, ROW_QBIAS, ROW_VBIAS, ROW_OBIAS, ROW_GAIN2, ROW_BIAS2 = range(8, 15)
SMALL = 128
ROW_PROB, ROW_EOUT, ROW_EIN = 16, 32, 40
AT_EIN, AT_EOUT, AT_HIGH, AT_LOW, AT_IMAGES = 16, 48, 56, 64, 72
CORES = 2
CHIPS = EXPERTS // CORES
BLOCK = 16
COL_T0, COL_T1, COL_R0, COL_R1, COL_K0, COL_K1, COL_LIVE = range(7)
VMEM_LIMIT = 60 * 1024 * 1024


def mm(a, b):
    return lax.dot_general(a, b, (((1,), (0,)), ((), ())), preferred_element_type=F32)


def mm_nt(a, b):
    return lax.dot_general(a, b, (((1,), (1,)), ((), ())), preferred_element_type=F32)


def mm_tn(a, b):
    return lax.dot_general(a, b, (((0,), (0,)), ((), ())), preferred_element_type=F32)


def load_padded(dst, src, seq_len, pad_len):
    for i in range(2):
        tail = (seq_len // 16) * 16
        dst[i * pad_len + tail : (i + 1) * pad_len, :] = jnp.zeros(
            (pad_len - tail, dst.shape[1]), dst.dtype
        )
        dst[i * pad_len : i * pad_len + seq_len, :] = src[i].astype(dst.dtype)


def load_table(facts, table, meta_ref, pad_len):
    for i in range(2):
        table[0 : meta_ref.shape[1], :] = meta_ref[i]
        facts[i * pad_len : (i + 1) * pad_len, :] = table[...].T


def norm_parts(x):
    mean = jnp.mean(x, -1, keepdims=True)
    centered = x - mean
    spread = jnp.mean(centered * centered, -1, keepdims=True)
    inv = lax.rsqrt(spread + EPSILON)
    return centered * inv, inv


def norm_back(d_out, xhat, inv, gain):
    d_hat = d_out * gain
    first = jnp.mean(d_hat, -1, keepdims=True)
    second = jnp.mean(d_hat * xhat, -1, keepdims=True)
    return inv * (d_hat - first - xhat * second)


def half_masks():
    lane = lax.broadcasted_iota(jnp.int32, (1, PAIR), 1)
    low = jnp.where(lane < HEAD_DIM, 1.0, 0.0)
    return low.astype(BF), (1.0 - low).astype(BF), lane < HEAD_DIM


def stack_heads(block, low, high):
    return jnp.concatenate([block * low, block * high], 0)


def forward_kernel(
    m0,
    seq_len,
    pad_len,
    assemble,
    cnt_ref,
    img_ref,
    cot_ref,
    meta_ref,
    first_ref,
    second_ref,
    xd_ref,
    qkv_ref,
    p_ref,
    att_ref,
    mid_ref,
    rp_ref,
    psum_ref,
    *rest,
):
    if assemble:
        w_ref, small_ref, xs, cs, facts, table = rest
    else:
        w_ref, small_ref = first_ref, second_ref
        xs, cs, facts, table = rest
    step = pl.program_id(0)
    width = xs.shape[1]
    alive = cnt_ref[0] > 2 * (m0 + step)

    @pl.when(step == 0)
    def _():
        psum_ref[...] = jnp.zeros_like(psum_ref)
        table[...] = jnp.zeros_like(table)
        if assemble:
            core = lax.rem(lax.axis_index("dp"), CORES)
            for ref, owner in ((first_ref, core), (second_ref, 1 - core)):
                for chip in range(CHIPS):
                    for z in range(ref.shape[1] // BLOCK):
                        plane = lax.bitwise_xor(lax.axis_index("dp") // EXPERTS, z)
                        at = plane * EXPERTS + chip * CORES + owner
                        at = pl.multiple_of(at * BLOCK, BLOCK)
                        w_ref[pl.ds(at, BLOCK), :] = ref[chip, z * BLOCK : (z + 1) * BLOCK, :]
            small_ref[...] = w_ref[:, 4 * width :].astype(F32).T

    @pl.when(jnp.logical_not(alive))
    def _():
        xd_ref[...] = jnp.zeros_like(xd_ref)

    @pl.when(alive)
    def _():
        load_padded(xs, img_ref, seq_len, pad_len)
        load_padded(cs, cot_ref, seq_len, pad_len)
        load_table(facts, table, meta_ref, pad_len)
        xhat, inv = norm_parts(xs[...])
        normed = (
            xhat * small_ref[ROW_GAIN1 : ROW_GAIN1 + 1, :] + small_ref[ROW_BIAS1 : ROW_BIAS1 + 1, :]
        ).astype(BF)
        for part, row in ((0, ROW_QBIAS), (1, None), (2, ROW_VBIAS)):
            cols = slice(part * width, (part + 1) * width)
            value = mm(normed, w_ref[:, cols])
            if row is not None:
                value = value + small_ref[row : row + 1, :]
            qkv_ref[0, :, cols] = value.astype(BF)
        low, high, low_mask = half_masks()
        key_ok = lax.broadcasted_iota(jnp.int32, (1, pad_len), 1) < seq_len
        for i in range(2):
            rows = slice(i * pad_len, (i + 1) * pad_len)
            for hp in range(HEADS // 2):
                at = hp * PAIR
                q = qkv_ref[0, rows, at : at + PAIR]
                k = qkv_ref[0, rows, width + at : width + at + PAIR]
                v = qkv_ref[0, rows, 2 * width + at : 2 * width + at + PAIR]
                s = mm_nt(stack_heads(q, low, high), k) * (HEAD_DIM**-0.5)
                s = jnp.where(key_ok, s, -1e30)
                e = jnp.exp(s - jnp.max(s, -1, keepdims=True))
                p = (e * (1.0 / jnp.sum(e, -1, keepdims=True))).astype(BF)
                p_ref[0, i, hp] = p
                o = mm(p, v)
                att_ref[0, rows, at : at + PAIR] = jnp.where(
                    low_mask, o[:pad_len], o[pad_len:]
                ).astype(BF)
        middle = (
            xs[...]
            + mm(att_ref[0], w_ref[:, 3 * width : 4 * width])
            + small_ref[ROW_OBIAS : ROW_OBIAS + 1, :]
        )
        mid_ref[0] = middle
        xhat2, inv2 = norm_parts(middle)
        mixed = (
            xhat2 * small_ref[ROW_GAIN2 : ROW_GAIN2 + 1, :]
            + small_ref[ROW_BIAS2 : ROW_BIAS2 + 1, :]
        ).astype(BF)
        logits = mm(mixed, w_ref[:, 4 * width : 4 * width + SMALL])
        lane = lax.broadcasted_iota(jnp.int32, (1, SMALL), 1)
        logits = jnp.where(lane < EXPERTS, logits, -1e30)
        e = jnp.exp(logits - jnp.max(logits, -1, keepdims=True))
        rp = e * (1.0 / jnp.sum(e, -1, keepdims=True))
        rp_ref[0] = rp
        live = facts[:, COL_LIVE : COL_LIVE + 1]
        psum_ref[0:1, :] += jnp.sum(rp * live, 0, keepdims=True)
        d_final = cs[...] * live
        lane_f = lane.astype(F32)
        weighted = []
        for route, kept in ((COL_R0, COL_K0), (COL_R1, COL_K1)):
            hot = lane_f == facts[:, route : route + 1]
            gate = jnp.sum(jnp.where(hot, rp, 0.0), -1, keepdims=True)
            gate = gate * facts[:, kept : kept + 1]
            weighted.append((gate * d_final).astype(BF))
        slot = lax.broadcasted_iota(jnp.int32, (DISPATCH * CAP, 1), 0).astype(F32)
        targets = facts[...].T
        for e_id in range(0, EXPERTS, DISPATCH):
            here = slot + float(e_id * CAP)
            sel0 = jnp.where(here == targets[COL_T0 : COL_T0 + 1, :], 1.0, 0.0)
            sel1 = jnp.where(here == targets[COL_T1 : COL_T1 + 1, :], 1.0, 0.0)
            shape = (DISPATCH, CAP, width)
            at = slice(e_id, e_id + DISPATCH)
            xd_ref[at, 0, 0] = mm((sel0 + sel1).astype(BF), mixed).astype(BF).reshape(shape)
            xd_ref[at, 1, 0] = (
                (mm(sel0.astype(BF), weighted[0]) + mm(sel1.astype(BF), weighted[1]))
                .astype(BF)
                .reshape(shape)
            )


def full_block(shape):
    return pl.BlockSpec(shape, lambda i: (0,) * len(shape))


def pack_kernel(in_ref, out_ref, pack_ref):
    width = out_ref.shape[2]
    half = out_ref.shape[1]
    for c in range(half // BLOCK):
        pack_ref[:, c * BLOCK : (c + 1) * BLOCK, :] = in_ref[:, :, c * width : (c + 1) * width]
    pack_ref[:, half:, :] = out_ref[...]


def pack_call(expert_in, expert_out):
    vm = pl.BlockSpec(memory_space=pltpu.VMEM)
    shape = (expert_out.shape[0], 2 * expert_out.shape[1], expert_out.shape[2])
    return pl.pallas_call(
        pack_kernel,
        in_specs=[vm] * 2,
        out_specs=vm,
        out_shape=jax.ShapeDtypeStruct(shape, BF),
        name="pack",
    )(expert_in, expert_out)


def prepare_kernel(
    cnt_ref,
    index_ref,
    qkv_ref,
    out_ref,
    router_ref,
    gain1_ref,
    bias1_ref,
    qv_ref,
    obias_ref,
    gain2_ref,
    bias2_ref,
    ein_ref,
    eout_ref,
    packed_ref,
    turned,
):
    rows, width = out_ref.shape
    packed_ref[:, 0 : 3 * width] = qkv_ref[...]
    packed_ref[:, 3 * width : 4 * width] = out_ref[...]
    turned[...] = jnp.zeros_like(turned)
    turned[0:EXPERTS, 0:rows] = router_ref[...].astype(F32)
    for row, ref in (
        (ROW_GAIN1, gain1_ref),
        (ROW_BIAS1, bias1_ref),
        (ROW_OBIAS, obias_ref),
        (ROW_GAIN2, gain2_ref),
        (ROW_BIAS2, bias2_ref),
    ):
        turned[row : row + 1, 0:rows] = ref[...].astype(F32)
    turned[ROW_QBIAS : ROW_VBIAS + 1, 0:rows] = qv_ref[...].astype(F32)
    turned[AT_EOUT : AT_EOUT + EXPERTS, 0:rows] = eout_ref[...].astype(F32)
    ein = ein_ref[...].astype(F32)
    for c in range(ein.shape[1] // rows):
        at = AT_EIN + c * EXPERTS
        turned[at : at + EXPERTS, 0:rows] = ein[:, c * rows : (c + 1) * rows]
    slots, top, seq_len = index_ref.shape
    chosen = index_ref[...]
    slot = lax.broadcasted_iota(jnp.int32, (slots, top, seq_len), 0)
    chosen = jnp.where(slot < cnt_ref[0], chosen, -1)
    for e in range(EXPERTS):
        hits = jnp.where(chosen == e, 1.0, 0.0)
        hits = jnp.sum(jnp.sum(hits, 0), -1, keepdims=True)
        hits = jnp.sum(hits, 0, keepdims=True)
        high = jnp.floor(hits * (1.0 / 128.0))
        turned[AT_HIGH + e : AT_HIGH + e + 1, :] = jnp.broadcast_to(high, (1, SMALL))
        turned[AT_LOW + e : AT_LOW + e + 1, :] = jnp.broadcast_to(hits - 128.0 * high, (1, SMALL))
    turned[AT_IMAGES : AT_IMAGES + 1, :] = jnp.full((1, SMALL), cnt_ref[0].astype(F32))
    turned[...] = turned[...].T
    packed_ref[:, 4 * width :] = turned[0:rows, :].astype(BF)


def prepare_call(count, *args):
    vm = pl.BlockSpec(memory_space=pltpu.VMEM)
    rows, width = args[2].shape
    return pl.pallas_call(
        prepare_kernel,
        in_specs=[pl.BlockSpec(memory_space=pltpu.SMEM)] + [vm] * len(args),
        out_specs=vm,
        out_shape=jax.ShapeDtypeStruct((rows, 4 * width + SMALL), BF),
        scratch_shapes=[pltpu.VMEM((SMALL, SMALL), F32)],
        name="prepare",
    )(count, *args)


def forward_call(m0, mbc, assemble, images, cotangent, count, meta, weights, small):
    seq_len, width = images.shape[1], images.shape[2]
    pad_len = meta.shape[2]
    rows = 2 * pad_len
    at = lambda i: i + m0
    mb = images.shape[0] // mbc
    made_here = []
    if assemble:
        made_here = [
            jax.ShapeDtypeStruct((width, weights.shape[2]), BF),
            jax.ShapeDtypeStruct((SMALL, width), F32),
        ]
    return pl.pallas_call(
        functools.partial(forward_kernel, m0, seq_len, pad_len, assemble),
        grid=(mbc,),
        in_specs=[
            pl.BlockSpec(memory_space=pltpu.SMEM),
            pl.BlockSpec((mb, seq_len, width), lambda i: (i, 0, 0)),
            pl.BlockSpec((mb, seq_len, width), lambda i: (i, 0, 0)),
            pl.BlockSpec((mb, 8, pad_len), lambda i: (at(i), 0, 0)),
            full_block(weights.shape),
            full_block(small.shape),
        ],
        out_specs=[
            pl.BlockSpec((EXPERTS, 2, 1, CAP, width), lambda i: (0, 0, i, 0, 0)),
            pl.BlockSpec((1, rows, 3 * width), lambda i: (i, 0, 0)),
            pl.BlockSpec((1, 2, HEADS // 2, rows, pad_len), lambda i: (i, 0, 0, 0, 0)),
            pl.BlockSpec((1, rows, width), lambda i: (i, 0, 0)),
            pl.BlockSpec((1, rows, width), lambda i: (i, 0, 0)),
            pl.BlockSpec((1, rows, SMALL), lambda i: (i, 0, 0)),
            full_block((8, SMALL)),
        ]
        + [full_block(made.shape) for made in made_here],
        out_shape=[
            jax.ShapeDtypeStruct((EXPERTS, 2, mbc, CAP, width), BF),
            jax.ShapeDtypeStruct((mbc, rows, 3 * width), BF),
            jax.ShapeDtypeStruct((mbc, 2, HEADS // 2, rows, pad_len), BF),
            jax.ShapeDtypeStruct((mbc, rows, width), BF),
            jax.ShapeDtypeStruct((mbc, rows, width), F32),
            jax.ShapeDtypeStruct((mbc, rows, SMALL), F32),
            jax.ShapeDtypeStruct((8, SMALL), F32),
        ]
        + made_here,
        scratch_shapes=[
            pltpu.VMEM((rows, width), F32),
            pltpu.VMEM((rows, width), F32),
            pltpu.VMEM((rows, SMALL), F32),
            pltpu.VMEM((SMALL, pad_len), F32),
        ],
        compiler_params=pltpu.CompilerParams(vmem_limit_bytes=VMEM_LIMIT),
        cost_estimate=pl.CostEstimate(
            flops=mbc * 8 * 10**9, bytes_accessed=mbc * 10 * 10**6, transcendentals=0
        ),
        name="dense_forward",
    )(count, images, cotangent, meta, weights, small)


GROUP = 4


def expert_kernel(
    m0,
    mbc,
    has_acc,
    last,
    cnt_ref,
    x_ref,
    w_ref,
    b1_ref,
    b2_ref,
    *rest,
):
    if has_acc:
        a1_ref, a2_ref, ab1_ref, ab2_ref = rest[:4]
        rest = rest[4:]
    if last:
        y_ref, pack_ref, gb1_ref, gb2_ref, s1, s2, order, xin, din, xout, dout = rest
    else:
        y_ref, s1, s2, gb1_ref, gb2_ref, order, xin, din, xout, dout = rest
    width = x_ref.shape[-1]
    ff = b1_ref.shape[1]
    half = w_ref.shape[1] // 2
    per_tile = width // half
    if has_acc:
        s1[...] = a1_ref[...]
        s2[...] = a2_ref[...]
        gb1_ref[...] = ab1_ref[...]
        gb2_ref[...] = ab2_ref[...]
    else:
        s1[...] = jnp.zeros_like(s1)
        s2[...] = jnp.zeros_like(s2)
        gb1_ref[...] = jnp.zeros_like(gb1_ref)
        gb2_ref[...] = jnp.zeros_like(gb2_ref)
    blocks = EXPERTS * mbc

    def is_live(b):
        return (cnt_ref[b // mbc] > 2 * (m0 + b % mbc)).astype(jnp.int32)

    live_total = jnp.int32(0)
    for b in range(blocks):
        live_total = live_total + is_live(b)
    head, tail = jnp.int32(0), live_total
    for b in range(blocks):
        flag = is_live(b)
        order[jnp.where(flag == 1, head, tail)] = b
        head = head + flag
        tail = tail + (1 - flag)

    def one_group(g, carry):
        for j in range(GROUP):
            b = order[g * GROUP + j]
            xin[j * CAP : (j + 1) * CAP, :] = x_ref[b // mbc, 0, b % mbc]
            din[j * CAP : (j + 1) * CAP, :] = x_ref[b // mbc, 1, b % mbc]
        rows_in, d_res = xin[...], din[...]
        gb2_ref[0:1, :] += jnp.sum(d_res.astype(F32), 0, keepdims=True)
        for f in range(ff // width):
            cols = slice(f * width, (f + 1) * width)
            w1 = w_ref[:, f * BLOCK : (f + 1) * BLOCK, :].reshape(width, width)
            w2 = w_ref[f * per_tile : (f + 1) * per_tile, half:, :].reshape(width, width)
            h = mm(rows_in, w1) + b1_ref[0:1, cols]
            bell = jnp.exp(-0.5 * h * h)
            t = 1.0 / (1.0 + (0.3275911 / math.sqrt(2.0)) * jnp.abs(h))
            poly = t * (
                0.5 * 0.254829592
                + t
                * (
                    0.5 * -0.284496736
                    + t * (0.5 * 1.421413741 + t * (0.5 * -1.453152027 + t * (0.5 * 1.061405429)))
                )
            )
            upper = poly * bell
            cdf = jnp.where(h < 0.0, upper, 1.0 - upper)
            act = (h * cdf).astype(BF)
            slope = cdf + h * bell * (1.0 / math.sqrt(2.0 * math.pi))
            d_act = mm_nt(d_res, w2)
            d_hid_f = (d_act * slope).astype(BF)
            gb1_ref[0:1, cols] += jnp.sum(d_hid_f.astype(F32), 0, keepdims=True)
            res = mm(act, w2)
            d_rows = mm_nt(d_hid_f, w1)
            if f == 0:
                xout[...] = res
                dout[...] = d_rows
            else:
                xout[...] += res
                dout[...] += d_rows
            s1[:, cols] += mm_tn(rows_in, d_hid_f)
            s2[cols, :] += mm_tn(act, d_res)
        for j in range(GROUP):
            b = order[g * GROUP + j]
            y_ref[b // mbc, 0, b % mbc] = (
                xout[j * CAP : (j + 1) * CAP, :] + b2_ref[0:1, :]
            ).astype(BF)
            y_ref[b // mbc, 1, b % mbc] = dout[j * CAP : (j + 1) * CAP, :].astype(BF)
        return carry

    lax.fori_loop(0, (live_total + GROUP - 1) // GROUP, one_group, 0)
    if last:
        blocks_of = width // BLOCK
        for f in range(ff // width):
            tile = s1[:, f * width : (f + 1) * width].astype(BF)
            pack_ref[:, f * BLOCK : (f + 1) * BLOCK, :] = tile.reshape(blocks_of, BLOCK, width)
        pack_ref[:, half:, :] = s2[...].astype(BF).reshape(blocks_of, half, width)


def expert_call(m0, mbc, last, counts, x, weights, b1, b2, acc):
    width, ff = weights.shape[2], b1.shape[1]
    if last:
        grads = [jax.ShapeDtypeStruct(weights.shape, BF)]
    else:
        grads = [jax.ShapeDtypeStruct((width, ff), F32), jax.ShapeDtypeStruct((ff, width), F32)]
    vm = pl.BlockSpec(memory_space=pltpu.VMEM)
    scratch = []
    if last:
        scratch += [pltpu.VMEM((width, ff), F32), pltpu.VMEM((ff, width), F32)]
    scratch += [
        pltpu.SMEM((EXPERTS * mbc,), jnp.int32),
        pltpu.VMEM((GROUP * CAP, width), BF),
        pltpu.VMEM((GROUP * CAP, width), BF),
        pltpu.VMEM((GROUP * CAP, width), F32),
        pltpu.VMEM((GROUP * CAP, width), F32),
    ]
    return pl.pallas_call(
        functools.partial(expert_kernel, m0, mbc, acc is not None, last),
        in_specs=[pl.BlockSpec(memory_space=pltpu.SMEM)] + [vm] * (4 + (0 if acc is None else 4)),
        out_specs=[vm] * (len(grads) + 3),
        out_shape=[
            jax.ShapeDtypeStruct(x.shape, BF),
            *grads,
            jax.ShapeDtypeStruct((8, ff), F32),
            jax.ShapeDtypeStruct((8, width), F32),
        ],
        scratch_shapes=scratch,
        compiler_params=pltpu.CompilerParams(vmem_limit_bytes=VMEM_LIMIT),
        cost_estimate=pl.CostEstimate(
            flops=mbc * 20 * 10**9, bytes_accessed=mbc * 10 * 10**6, transcendentals=0
        ),
        name="expert_both",
    )(counts, x, weights, b1, b2, *(() if acc is None else acc))


def backward_kernel(
    m0,
    seq_len,
    pad_len,
    has_acc,
    last,
    cnt_ref,
    img_ref,
    cot_ref,
    meta_ref,
    y_ref,
    qkv_hbm,
    p_hbm,
    att_ref,
    mid_ref,
    rp_ref,
    coef_ref,
    w_hbm,
    small_ref,
    extra_ref,
    *rest,
):
    if has_acc:
        accw_ref, accs_ref = rest[:2]
        rest = rest[4:]
    if last:
        out_ref, grad_ref, pack_ref, *rest = rest
        gw_ref, gs_ref, earlier, sem = rest[-4:]
        rest = rest[:-4]
    else:
        out_ref, grad_ref, gw_ref, gs_ref, *rest = rest
    xs, cs, dq, facts, table, qkv_all, p_all, w_ref, sems = rest
    step = pl.program_id(0)
    width = xs.shape[1]
    alive = cnt_ref[0] > 2 * (m0 + step)
    qkv_ref, p_ref = qkv_all.at[pl.ds(step, 1)], p_all.at[pl.ds(step, 1)]
    steps = qkv_all.shape[0]

    def late(which, at):
        if which == "rest":
            cols = pl.ds(3 * width, width + SMALL)
            return pltpu.make_async_copy(w_hbm.at[:, cols], w_ref.at[:, cols], sems.at[2 * steps])
        if which == "first":
            cols = pl.ds(0, 3 * width)
            return pltpu.make_async_copy(
                w_hbm.at[:, cols], w_ref.at[:, cols], sems.at[2 * steps + 1]
            )
        if which == "qkv":
            return pltpu.make_async_copy(qkv_hbm.at[at], qkv_all.at[at], sems.at[at])
        return pltpu.make_async_copy(p_hbm.at[at], p_all.at[at], sems.at[steps + at])


    @pl.when(step == 0)
    def _():
        late("rest", 0).start()
        for at in range(steps):
            late("qkv", at).start()
            late("p", at).start()
        late("first", 0).start()
        table[...] = jnp.zeros_like(table)
        gw_ref[...] = jnp.zeros_like(gw_ref)
        if has_acc:
            pltpu.make_async_copy(accw_ref, earlier, sem).start()
            gs_ref[...] = accs_ref[...]
        else:
            gs_ref[...] = jnp.zeros_like(gs_ref)

    @pl.when(jnp.logical_not(alive))
    def _():
        out_ref[...] = jnp.zeros_like(out_ref)
        grad_ref[...] = jnp.zeros_like(grad_ref)
        late("qkv", step).wait()
        late("p", step).wait()

        @pl.when(step == 0)
        def _():
            late("rest", 0).wait()
            late("first", 0).wait()

    def add_row(row, value):
        gs_ref[row : row + 1, :] += jnp.sum(value, 0, keepdims=True)

    @pl.when(alive)
    def _():
        load_padded(xs, img_ref, seq_len, pad_len)
        load_padded(cs, cot_ref, seq_len, pad_len)
        load_table(facts, table, meta_ref, pad_len)
        rows = xs.shape[0]
        live = facts[:, COL_LIVE : COL_LIVE + 1]
        d_final = cs[...] * live
        middle = mid_ref[0]
        rp = rp_ref[0]
        lane = lax.broadcasted_iota(jnp.int32, (1, SMALL), 1)
        lane_f = lane.astype(F32)
        slot = lax.broadcasted_iota(jnp.int32, (1, EXPERTS * CAP), 1).astype(F32)
        res = y_ref[:, 0, 0].reshape(EXPERTS * CAP, width)
        d_rows = y_ref[:, 1, 0].reshape(EXPERTS * CAP, width)
        final = middle
        d_prob = coef_ref[0:1, :] * live
        sel_all = None
        for target, route, kept in ((COL_T0, COL_R0, COL_K0), (COL_T1, COL_R1, COL_K1)):
            sel = jnp.where(slot == facts[:, target : target + 1], 1.0, 0.0).astype(BF)
            sel_all = sel if sel_all is None else sel_all + sel
            picked = mm(sel, res)
            keep = facts[:, kept : kept + 1]
            hot = lane_f == facts[:, route : route + 1]
            gate = jnp.sum(jnp.where(hot, rp, 0.0), -1, keepdims=True) * keep
            final = final + gate * picked
            d_gate = jnp.sum(picked * d_final, -1, keepdims=True) * keep
            d_prob = d_prob + jnp.where(hot, d_gate, 0.0)
        final = final * live
        for i in range(2):
            out_ref[i] = final[i * pad_len : i * pad_len + seq_len, :].astype(BF)
        d_mixed = mm(sel_all, d_rows)

        @pl.when(step == 0)
        def _():
            late("rest", 0).wait()

        d_logits = (rp * (d_prob - jnp.sum(rp * d_prob, -1, keepdims=True))).astype(BF)
        d_mixed = d_mixed + mm_nt(d_logits, w_ref[:, 4 * width : 4 * width + SMALL])
        gain2 = small_ref[ROW_GAIN2 : ROW_GAIN2 + 1, :]
        xhat2, inv2 = norm_parts(middle)
        mixed = (xhat2 * gain2 + small_ref[ROW_BIAS2 : ROW_BIAS2 + 1, :]).astype(BF)
        gs_ref[0:EXPERTS, :] += mm_tn(d_logits, mixed)[0:EXPERTS, :]
        add_row(ROW_GAIN2, d_mixed * xhat2)
        add_row(ROW_BIAS2, d_mixed)
        d_middle = d_final + norm_back(d_mixed, xhat2, inv2, gain2)
        add_row(ROW_OBIAS, d_middle)
        cs[...] = d_middle
        d_branch = d_middle.astype(BF)
        gw_ref[:, 3 * width : 4 * width] += mm_tn(att_ref[0], d_branch)
        d_att_all = mm_nt(d_branch, w_ref[:, 3 * width : 4 * width]).astype(BF)
        late("qkv", step).wait()
        late("p", step).wait()
        low, high, low_mask = half_masks()
        scale = HEAD_DIM**-0.5
        for i in range(2):
            span = slice(i * pad_len, (i + 1) * pad_len)
            for hp in range(HEADS // 2):
                at = hp * PAIR
                q = qkv_ref[0, span, at : at + PAIR]
                k = qkv_ref[0, span, width + at : width + at + PAIR]
                v = qkv_ref[0, span, 2 * width + at : 2 * width + at + PAIR]
                d_att = stack_heads(d_att_all[span, at : at + PAIR], low, high)
                p = p_ref[0, i, hp]
                pf = p.astype(F32)
                d_attn = mm_nt(d_att, v)
                d_s = (pf * (d_attn - jnp.sum(pf * d_attn, -1, keepdims=True))).astype(BF)
                d_v = mm_tn(p, d_att)
                d_k = mm_tn(d_s, stack_heads(q, low, high)) * scale
                d_q = mm(d_s, k) * scale
                dq[span, at : at + PAIR] = jnp.where(
                    low_mask, d_q[:pad_len], d_q[pad_len:]
                ).astype(BF)
                dq[span, width + at : width + at + PAIR] = d_k.astype(BF)
                dq[span, 2 * width + at : 2 * width + at + PAIR] = d_v.astype(BF)
        gain1 = small_ref[ROW_GAIN1 : ROW_GAIN1 + 1, :]
        xhat, inv = norm_parts(xs[...])
        normed = (xhat * gain1 + small_ref[ROW_BIAS1 : ROW_BIAS1 + 1, :]).astype(BF)
        add_row(ROW_QBIAS, dq[:, 0:width].astype(F32))
        add_row(ROW_VBIAS, dq[:, 2 * width : 3 * width].astype(F32))
        gw_ref[:, 0 : 3 * width] += mm_tn(normed, dq[...])

        @pl.when(step == 0)
        def _():
            late("first", 0).wait()

        d_normed = mm_nt(dq[...], w_ref[:, 0 : 3 * width])
        add_row(ROW_GAIN1, d_normed * xhat)
        add_row(ROW_BIAS1, d_normed)
        d_tok = cs[...] + norm_back(d_normed, xhat, inv, gain1)
        for i in range(2):
            grad_ref[i] = d_tok[i * pad_len : i * pad_len + seq_len, :].astype(BF)

    if last:

        @pl.when(step == pl.num_programs(0) - 1)
        def _():
            if has_acc:
                pltpu.make_async_copy(accw_ref, earlier, sem).wait()
                gw_ref[...] += earlier[...]
            small_part = (gs_ref[...] + extra_ref[...]).T.astype(BF)
            for b in range(width // BLOCK):
                at = slice(b * BLOCK, (b + 1) * BLOCK)
                core = b % CORES
                if len(pack_ref.shape) == 4:
                    ref = pack_ref.at[core, b // CORES]
                else:
                    ref = pack_ref.at[at]
                ref[:, 0 : 4 * width] = gw_ref[at, :].astype(BF)
                ref[:, 4 * width :] = small_part[at, :]


def backward_call(
    m0,
    mbc,
    last,
    own_rows,
    images,
    cotangent,
    count,
    meta,
    back,
    saved,
    coef,
    weights,
    small,
    extra,
    acc,
):
    seq_len, width = images.shape[1], images.shape[2]
    pad_len = meta.shape[2]
    rows = 2 * pad_len
    mb = images.shape[0] // mbc
    qkv, probs, att, mid, rp = saved
    at = lambda i: i + m0
    image_block = pl.BlockSpec((mb, seq_len, width), lambda i: (i, 0, 0))
    made_block = pl.BlockSpec((mb, seq_len, width), lambda i: (at(i), 0, 0))
    made = jax.ShapeDtypeStruct((mb * MICRO, seq_len, width), BF)
    in_specs = [
        pl.BlockSpec(memory_space=pltpu.SMEM),
        image_block,
        image_block,
        pl.BlockSpec((mb, 8, pad_len), lambda i: (at(i), 0, 0)),
        pl.BlockSpec((EXPERTS, 2, 1, CAP, width), lambda i: (0, 0, i, 0, 0)),
        pl.BlockSpec(memory_space=pl.ANY),
        pl.BlockSpec(memory_space=pl.ANY),
        pl.BlockSpec((1, rows, width), lambda i: (i, 0, 0)),
        pl.BlockSpec((1, rows, width), lambda i: (i, 0, 0)),
        pl.BlockSpec((1, rows, SMALL), lambda i: (i, 0, 0)),
        full_block(coef.shape),
        pl.BlockSpec(memory_space=pl.ANY),
        full_block(small.shape),
        full_block(extra.shape),
    ]
    args = [count, images, cotangent, meta, back, qkv, probs, att, mid, rp]
    args += [coef, weights, small, extra]
    aliases = {}
    if acc is not None:
        base = len(args)
        in_specs += [pl.BlockSpec(memory_space=pl.ANY), full_block(acc[1].shape)]
        in_specs += [pl.BlockSpec(memory_space=pl.ANY)] * 2
        args += list(acc)
        aliases = {base + 2: 0, base + 3: 1}
    sums = [(width, 4 * width), (SMALL, width)]
    pack_shape = (width, weights.shape[1])
    if own_rows == BLOCK:
        pack_shape = (CORES, width // (CORES * BLOCK), BLOCK, weights.shape[1])
    if last:
        grads = [jax.ShapeDtypeStruct(pack_shape, BF)]
        held = [pltpu.VMEM(shape, F32) for shape in sums]
        held += [pltpu.VMEM(sums[0], F32), pltpu.SemaphoreType.DMA]
    else:
        grads = [jax.ShapeDtypeStruct(shape, F32) for shape in sums]
        held = []
    return pl.pallas_call(
        functools.partial(backward_kernel, m0, seq_len, pad_len, acc is not None, last),
        grid=(mbc,),
        in_specs=in_specs,
        out_specs=[
            made_block,
            made_block,
        ]
        + [full_block(g.shape) for g in grads],
        out_shape=[
            made,
            made,
        ]
        + grads,
        scratch_shapes=[
            pltpu.VMEM((rows, width), F32),
            pltpu.VMEM((rows, width), F32),
            pltpu.VMEM((rows, 3 * width), BF),
            pltpu.VMEM((rows, SMALL), F32),
            pltpu.VMEM((SMALL, pad_len), F32),
            pltpu.VMEM(qkv.shape, BF),
            pltpu.VMEM(probs.shape, BF),
            pltpu.VMEM(weights.shape, BF),
            pltpu.SemaphoreType.DMA((2 * mbc + 2,)),
        ]
        + held,
        input_output_aliases=aliases,
        compiler_params=pltpu.CompilerParams(vmem_limit_bytes=VMEM_LIMIT),
        cost_estimate=pl.CostEstimate(
            flops=mbc * 20 * 10**9, bytes_accessed=mbc * 10 * 10**6, transcendentals=0
        ),
        name="dense_backward",
    )(*args)


def finish_kernel(count, got_ref, bal_ref, *refs):
    experts, refs = refs[:count], refs[count:]
    qkv_ref, out_ref, router_ref, gain1_ref, bias1_ref, qv_ref, obias_ref = refs[:7]
    gain2_ref, bias2_ref, ein_ref, eout_ref, balance_ref, *refs = refs[7:]
    turned = refs[-1]
    if experts:
        in_ref, back_ref = refs[:2]
        half, wide_of = back_ref.shape[1:]
        for r, block in enumerate(experts):
            e = lax.bitwise_xor(lax.rem(lax.axis_index("dp"), EXPERTS), r)
            for c in range(half // BLOCK):
                in_ref[e, :, c * wide_of : (c + 1) * wide_of] = block[
                    c * BLOCK : (c + 1) * BLOCK, :
                ].astype(F32)
            back_ref[e] = block[half:, :].astype(F32)
    sources, rows, wide = got_ref.shape
    width = out_ref.shape[1]
    whole = got_ref[0].astype(F32)
    for source in range(1, sources):
        whole = whole + got_ref[source].astype(F32)
    qkv_ref[...] = whole[:, : 3 * width]
    out_ref[...] = whole[:, 3 * width : 4 * width]
    turned[...] = jnp.zeros_like(turned)
    turned[0:rows, :] = whole[:, 4 * width :]
    balance_ref[...] = jnp.sum(turned[0:1, :] * bal_ref[0:1, :], -1, keepdims=True)
    turned[...] = turned[...].T
    router_ref[...] = turned[0:EXPERTS, 0:rows]
    for row, ref in (
        (ROW_GAIN1, gain1_ref),
        (ROW_BIAS1, bias1_ref),
        (ROW_OBIAS, obias_ref),
        (ROW_GAIN2, gain2_ref),
        (ROW_BIAS2, bias2_ref),
    ):
        ref[...] = turned[row : row + 1, 0:rows]
    qv_ref[...] = turned[ROW_QBIAS : ROW_VBIAS + 1, 0:rows]
    eout_ref[...] = turned[ROW_EOUT : ROW_EOUT + EXPERTS, 0:rows]
    for c in range(ein_ref.shape[1] // rows):
        at = ROW_EIN + c * EXPERTS
        ein_ref[:, c * rows : (c + 1) * rows] = turned[at : at + EXPERTS, 0:rows]


def finish_call(got, bal, experts, width, ff_rows):
    rows = got.shape[1]
    shapes = [
        (rows, 3 * width),
        (rows, width),
        (EXPERTS, rows),
        (1, rows),
        (1, rows),
        (2, rows),
        (1, rows),
        (1, rows),
        (1, rows),
        (EXPERTS, ff_rows),
        (EXPERTS, rows),
        (1, 1),
    ]
    if experts:
        half = experts[0].shape[0] // 2
        shapes += [(EXPERTS, BLOCK, half // BLOCK * width), (EXPERTS, half, width)]
    vm = pl.BlockSpec(memory_space=pltpu.VMEM)
    return pl.pallas_call(
        functools.partial(finish_kernel, len(experts)),
        in_specs=[vm] * (2 + len(experts)),
        out_specs=[vm] * len(shapes),
        out_shape=[jax.ShapeDtypeStruct(shape, F32) for shape in shapes],
        scratch_shapes=[pltpu.VMEM((SMALL, SMALL), F32)],
        name="finish",
    )(got, bal, *experts)


def shards(
    total,
    images,
    image_count,
    expert_index,
    expert_slot,
    keep,
    cotangent,
    ln1_gain,
    ln1_bias,
    qkv_weight,
    qv_bias,
    out_weight,
    out_bias,
    ln2_gain,
    ln2_bias,
    router_weight,
    expert_in,
    expert_in_bias,
    expert_out,
    expert_out_bias,
):
    slots, seq_len, width = images.shape
    planes = total // EXPERTS
    rows = width // total
    ff = expert_in.shape[2]
    ff_rows = ff // total
    mb = slots // MICRO
    pad_len = -(-seq_len // 16) * 16
    plane_groups = [[z * EXPERTS + p for p in range(EXPERTS)] for z in range(planes)]
    core_groups = [
        [z * EXPERTS + c * CORES + k for c in range(CHIPS)]
        for z in range(planes)
        for k in range(CORES)
    ]
    far_groups = [[CORES * i + k for i in range(total // CORES)] for k in range(CORES)]
    chip_groups = [[CORES * i + k for k in range(CORES)] for i in range(total // CORES)]
    z_groups = [[z * EXPERTS + p for z in range(planes)] for p in range(EXPERTS)]

    def plane_swap(v):
        return lax.all_to_all(v, "dp", 0, 0, tiled=True, axis_index_groups=plane_groups)

    def z_swap(v):
        return lax.all_to_all(v, "dp", 0, 0, tiled=True, axis_index_groups=z_groups)

    def z_gather(v):
        return lax.all_gather(v, "dp", axis=0, tiled=True, axis_index_groups=z_groups)

    parts = ff // width
    if rows == BLOCK:
        expert_pack = pack_call(expert_in, expert_out)
    else:
        expert_pack = jnp.concatenate(
            [
                expert_in.reshape(EXPERTS, rows, parts, width)
                .transpose(0, 2, 1, 3)
                .reshape(EXPERTS, ff_rows, width),
                expert_out,
            ],
            1,
        )
    expert_pack = plane_swap(expert_pack)

    live_img = (jnp.arange(slots) < image_count[0]).astype(F32)
    live_tok = jnp.broadcast_to(live_img[:, None, None], (slots, seq_len, 1))
    if rows == BLOCK:
        vectors = [v[None] for v in (ln1_gain, ln1_bias, out_bias, ln2_gain, ln2_bias)]
        packed = prepare_call(
            image_count,
            expert_index.transpose(0, 2, 1),
            qkv_weight,
            out_weight,
            router_weight.T,
            vectors[0],
            vectors[1],
            qv_bias,
            *vectors[2:],
            expert_in_bias,
            expert_out_bias,
        )
    else:
        hits = (expert_index[..., None] == jnp.arange(EXPERTS)).astype(F32) * live_tok[..., None]
        local_counts = jnp.sum(hits, axis=(0, 1, 2))
        high = jnp.floor(local_counts * (1.0 / 128.0))
        told = jnp.concatenate([high, local_counts - 128.0 * high, image_count.astype(F32)])
        small_cols = jnp.concatenate(
            [
                router_weight,
                ln1_gain[:, None],
                ln1_bias[:, None],
                qv_bias.T,
                out_bias[:, None],
                ln2_gain[:, None],
                ln2_bias[:, None],
                jnp.zeros((rows, 1), BF),
                expert_in_bias.reshape(EXPERTS, parts, rows).transpose(2, 1, 0).reshape(rows, -1),
                expert_out_bias.T,
                jnp.broadcast_to(told.astype(BF)[None], (rows, 2 * EXPERTS + 1)),
            ],
            1,
        )
        small_cols = jnp.pad(small_cols, ((0, 0), (0, SMALL - small_cols.shape[1])))
        packed = jnp.concatenate([qkv_weight, out_weight, small_cols], 1)
    wide = packed.shape[1]
    if rows == BLOCK:
        pieces = [packed]
        for z in range(1, planes):
            pieces.append(
                lax.ppermute(packed, "dp", [(i, i ^ (z * EXPERTS)) for i in range(total)])
            )
        packed = jnp.concatenate(pieces, 0)
    else:
        packed = z_gather(packed)
    spans = []
    for size in CHUNKS:
        spans.append((sum(span[1] for span in spans), size))
    held = {
        m0: [v[m0 * mb : (m0 + mbc) * mb] for v in (images, cotangent)] for m0, mbc in spans
    }
    packed = jnp.broadcast_to(packed[None], (CHIPS,) + packed.shape)
    packed, expert_pack = lax.optimization_barrier((packed, expert_pack))
    first = lax.all_to_all(
        packed,
        "dp",
        0,
        0,
        tiled=True,
        axis_index_groups=core_groups,
    )
    second = lax.ppermute(first, "dp", [(i, i ^ 1) for i in range(total)])
    me = lax.axis_index("dp")
    if rows != BLOCK:
        even = me % CORES == 0
        both = jnp.stack([jnp.where(even, first, second), jnp.where(even, second, first)], 1)
        first = (
            both.reshape(CHIPS, CORES, planes, rows, wide)
            .transpose(2, 0, 1, 3, 4)
            .reshape(width, wide)
        )
        second = first[:, 4 * width :].astype(F32).T

    index_t, slot_t, keep_t = (v.transpose(0, 2, 1) for v in (expert_index, expert_slot, keep))
    target = jnp.where(keep_t == 1, index_t * CAP + slot_t, -1).astype(F32)
    live_row = jnp.broadcast_to(live_img[:, None, None], (slots, 1, seq_len))
    flags = jnp.concatenate(
        [index_t.astype(F32), keep_t.astype(F32), live_row, jnp.zeros_like(live_row)], 1
    )
    beyond = ((0, 0), (0, 0), (0, pad_len - seq_len))
    meta = jnp.concatenate(
        [jnp.pad(target, beyond, constant_values=-1.0), jnp.pad(flags, beyond)], 1
    )

    expert_pack = z_gather(expert_pack)
    if rows != BLOCK:
        blocks = width // BLOCK
        expert_pack = jnp.concatenate(
            [
                expert_pack[:, :ff_rows]
                .reshape(blocks, total // blocks, parts, rows, width)
                .transpose(0, 2, 1, 3, 4)
                .reshape(blocks, parts * BLOCK, width),
                expert_pack[:, ff_rows:].reshape(blocks, parts * BLOCK, width),
            ],
            1,
        )

    saved, sent, prob_sums = [], [], []
    for m0, mbc in spans:
        assemble = m0 == 0 and rows == BLOCK
        xd, qkv, probs, att, mid, rp, prob, *made = forward_call(
            m0, mbc, assemble, *held[m0], image_count, meta, first, second
        )
        if assemble:
            first, second = made
        saved.append((qkv, probs, att, mid, rp))
        prob_sums.append(prob[0, :EXPERTS])
        sent.append(plane_swap(xd))
    weights = first
    small, _ = lax.optimization_barrier((second, prob_sums[-1]))

    in_bias = small[AT_EIN : AT_EIN + parts * EXPERTS].reshape(parts, EXPERTS, width)
    in_bias = lax.dynamic_index_in_dim(in_bias, me % EXPERTS, 1, keepdims=False)
    in_bias = in_bias.reshape(parts, total, rows).transpose(1, 0, 2).reshape(1, ff)
    out_bias_e = lax.dynamic_slice_in_dim(small, AT_EOUT + me % EXPERTS, 1, 0)
    sums = jnp.sum(small[AT_HIGH : AT_IMAGES + 1], 1) * (1.0 / rows)
    counts_all = sums[:EXPERTS] * 128.0 + sums[EXPERTS : 2 * EXPERTS]
    live_total = sums[2 * EXPERTS] * float(seq_len)
    plane_counts = lax.dynamic_slice_in_dim(
        small[AT_IMAGES], (me // EXPERTS) * (EXPERTS * rows), EXPERTS * rows, 0
    )
    plane_counts = plane_counts.reshape(EXPERTS, rows)[:, 0].astype(jnp.int32)
    coef = jnp.pad(BALANCE_WEIGHT * EXPERTS * counts_all / live_total, (0, SMALL - EXPERTS))
    coef = jnp.broadcast_to(coef[None], (8, SMALL))
    in_bias = jnp.broadcast_to(in_bias, (8, ff))
    out_bias_e = jnp.broadcast_to(out_bias_e, (8, width))

    acc = None
    back = []
    for (m0, mbc), rows_in in zip(spans, sent):
        y, *acc = expert_call(
            m0,
            mbc,
            m0 + mbc == MICRO,
            plane_counts,
            rows_in,
            expert_pack,
            in_bias,
            out_bias_e,
            acc,
        )
        back.append(plane_swap(y))
    expert_grads, gb1, gb2 = acc

    if rows != BLOCK:
        expert_grads = jnp.concatenate(
            [
                expert_grads[:, : parts * BLOCK]
                .reshape(blocks, parts, total // blocks, rows, width)
                .transpose(0, 2, 1, 3, 4)
                .reshape(total, ff_rows, width),
                expert_grads[:, parts * BLOCK :].reshape(total, ff_rows, width),
            ],
            1,
        )
    expert_grads = lax.psum_scatter(
        expert_grads, "dp", scatter_dimension=0, tiled=True, axis_index_groups=z_groups
    )
    if rows == BLOCK:
        place = me % EXPERTS
        blocks_in = []
        for r in range(EXPERTS):
            block = lax.dynamic_index_in_dim(expert_grads, place ^ r, 0, keepdims=False)
            if r:
                block = lax.ppermute(block, "dp", [(i, i ^ r) for i in range(total)])
            blocks_in.append(block)
    else:
        blocks_in = []
        expert_grads = plane_swap(expert_grads).astype(F32)
        expert_in_grad = (
            expert_grads[:, :ff_rows]
            .reshape(EXPERTS, parts, rows, width)
            .transpose(0, 2, 1, 3)
            .reshape(EXPERTS, rows, ff)
        )
        expert_out_grad = expert_grads[:, ff_rows:]

    prob_sum = prob_sums[0]
    for piece in prob_sums[1:]:
        prob_sum = prob_sum + piece
    p_hi = prob_sum.astype(BF).astype(F32)
    mine = (jnp.arange(EXPERTS) == me % EXPERTS).astype(F32)
    e_in = gb1[0].reshape(total, parts, rows).transpose(1, 0, 2).reshape(parts, 1, width)
    extra = jnp.concatenate(
        [
            jnp.zeros((ROW_PROB, width), F32),
            jnp.broadcast_to(
                jnp.concatenate([p_hi, prob_sum - p_hi])[:, None], (2 * EXPERTS, width)
            ),
            mine[:, None] * gb2[0:1],
            (mine[None, :, None] * e_in).reshape(parts * EXPERTS, width),
            jnp.zeros((SMALL - ROW_EIN - parts * EXPERTS, width), F32),
        ],
        0,
    )

    bal = EXPERTS * counts_all / live_total / live_total
    bal = jnp.concatenate([jnp.zeros((ROW_PROB,), F32), bal, bal])
    bal = jnp.broadcast_to(jnp.pad(bal, (0, SMALL - bal.shape[0]))[None], (8, SMALL))
    extra, bal = lax.optimization_barrier((extra, bal))

    acc = None
    for (m0, mbc), returned, kept in zip(spans, back, saved):
        block_out, image_grad, *acc = backward_call(
            m0,
            mbc,
            m0 + mbc == MICRO,
            rows,
            *held[m0],
            image_count,
            meta,
            returned,
            kept,
            coef,
            weights,
            small,
            extra,
            None if acc is None else (*acc, block_out, image_grad),
        )

    grads = acc[0]
    if rows != BLOCK:
        grads = grads.reshape(total // CORES, CORES, rows, wide).transpose(1, 0, 2, 3)
    grads = lax.all_to_all(grads, "dp", 0, 0, tiled=True, axis_index_groups=chip_groups)
    grads = jnp.sum(grads.astype(F32), 0).astype(BF)
    grads = lax.all_to_all(
        grads.reshape(total // CORES, rows, wide),
        "dp",
        0,
        0,
        tiled=True,
        axis_index_groups=far_groups,
    )
    (
        qkv_grad,
        out_grad,
        router_grad,
        gain1_grad,
        bias1_grad,
        qv_grad,
        obias_grad,
        gain2_grad,
        bias2_grad,
        ein_grad,
        eout_grad,
        balance,
        *expert_pair,
    ) = finish_call(grads, bal, blocks_in, width, ff_rows)
    if blocks_in:
        expert_in_grad, expert_out_grad = expert_pair
    return (
        block_out,
        image_grad,
        balance.reshape(()),
        gain1_grad.reshape(rows),
        bias1_grad.reshape(rows),
        qkv_grad,
        qv_grad,
        out_grad,
        obias_grad.reshape(rows),
        gain2_grad.reshape(rows),
        bias2_grad.reshape(rows),
        router_grad.T,
        expert_in_grad,
        ein_grad,
        expert_out_grad,
        eout_grad,
    )


def solution(mesh):
    placed = (
        P("dp", None, None),
        P("dp"),
        P("dp", None, None),
        P("dp", None, None),
        P("dp", None, None),
        P("dp", None, None),
        P("dp"),
        P("dp"),
        P("dp", None),
        P(None, "dp"),
        P("dp", None),
        P("dp"),
        P("dp"),
        P("dp"),
        P("dp", None),
        P(None, "dp", None),
        P(None, "dp"),
        P(None, "dp", None),
        P(None, "dp"),
    )
    return jax.shard_map(
        functools.partial(shards, mesh.shape["dp"]),
        mesh=mesh,
        in_specs=placed,
        out_specs=(
            P("dp", None, None),
            P("dp", None, None),
            P(),
            P("dp"),
            P("dp"),
            P("dp", None),
            P(None, "dp"),
            P("dp", None),
            P("dp"),
            P("dp"),
            P("dp"),
            P("dp", None),
            P(None, "dp", None),
            P(None, "dp"),
            P(None, "dp", None),
            P(None, "dp"),
        ),
        check_vma=False,
    )
```

profile of v0, /device:TPU:0, one launch (start us, length us, event | category | flops | bytes accessed | tf_op | source)
XLA Modules:
  0.0 361.6 jit_solution(11438017668050558886)
XLA Ops:
  7.2 2.2 pack.1
  9.4 5.2 %all-to-all-start = ((bf16[8,128,512]{2,1,0:T(8,128)(2,1)}), bf16[8,128,512]{2,1,0:T(8,128)(2,1)S(1)}, u32[]{:S(2)}, u32[]{:S(2)}) async-start(bf16[8,128,512]{2,1,0:T(8,128)(2,1)} %pack.1), calls=%async_computation | async-start | bytes 2097152 | tf_op jit(solution)/shard_map/all_to_all | solution.py:905
  17.1 3.6 collective-permute-start.2
  21.5 2.6 collective-permute-done.2
  24.0 3.3 collective-permute-done.1
  28.3 1.7 all-to-all-done
  31.2 4.3 %all-to-all-start.1 = ((bf16[4,64,2176]{2,1,0:T(8,128)(2,1)}), bf16[4,64,2176]{2,1,0:T(8,128)(2,1)}, u32[]{:S(2)}, u32[]{:S(2)}) async-start(bf16[4,64,2176]{2,1,0:T(8,128)(2,1)} %broadcast_in_dim.82), calls=%async_computation.1 | async-start | bytes 2228224 | tf_op jit(solution)/shard_map/all_to_all | solution.py:986
  38.8 10.3 %all-to-all-done.1.first_ref = bf16[4,64,2176]{2,1,0:T(8,128)(2,1)} async-done(((bf16[4,64,2176]{2,1,0:T(8,128)(2,1)}), bf16[4,64,2176]{2,1,0:T(8,128)(2,1)}, u32[]{:S(2)}, u32[]{:S(2)}) %all-to-all-start.1) | async-done | bytes 1114144 | tf_op jit(solution)/shard_map/all_to_all | solution.py:986
  50.0 2.1 collective-permute-done.3.second_ref
  53.1 16.8 %dense_forward.2 = (bf16[8,2,2,128,512]{4,3,2,1,0:T(8,128)(2,1)}, bf16[2,416,1536]{2,1,0:T(8,128)(2,1)}, bf16[2,2,4,416,208]{4,3,2,1,0:T(8,128)(2,1)}, bf16[2,41...) custom-call(s32[1]{0:T(128)} %copy.72.cnt_ref, ...), custom_call_target="tpu_custom_call" | custom-call | flops 16000000000 | bytes 20000000 | tf_op jit(solution)/shard_map/dense_forward/pallas_call | solution.py:314
  69.9 5.1 %all-to-all-start.3 = ((bf16[8,2,2,128,512]{4,3,2,1,0:T(8,128)(2,1)}), bf16[8,2,2,128,512]{4,3,2,1,0:T(8,128)(2,1)}, u32[]{:S(2)}, u32[]{:S(2)}) async-start(bf16[8,2,2,128,512]{4,3,2,1,0:T(8,128)(2,1)} %get-tuple-element.74), calls=%async_computation.3 | async-start | bytes 8388608 | tf_op jit(solution)/shard_map/all_to_all | solution.py:905
  82.7 7.0 %dense_forward.3 = (bf16[8,2,2,128,512]{4,3,2,1,0:T(8,128)(2,1)}, bf16[2,416,1536]{2,1,0:T(8,128)(2,1)}, bf16[2,2,4,416,208]{4,3,2,1,0:T(8,128)(2,1)}, bf16[2,41...) custom-call(s32[1]{0:T(128)} %copy.72.cnt_ref, ...), custom_call_target="tpu_custom_call" | custom-call | flops 16000000000 | bytes 20000000 | tf_op jit(solution)/shard_map/dense_forward/pallas_call | solution.py:314
  91.2 32.8 %all-to-all-done.3.x_ref = bf16[8,2,2,128,512]{4,3,2,1,0:T(8,128)(2,1)} async-done(((bf16[8,2,2,128,512]{4,3,2,1,0:T(8,128)(2,1)}), bf16[8,2,2,128,512]{4,3,2,1,0:T(8,128)(2,1)}, u32[]{:S(2)}, u32[]{:S(2)}) %all-to-all-start.3) | async-done | bytes 4194336 | tf_op jit(solution)/shard_map/all_to_all | solution.py:905
  124.1 4.6 %all-to-all-start.2 = ((bf16[8,2,2,128,512]{4,3,2,1,0:T(8,128)(2,1)}), bf16[8,2,2,128,512]{4,3,2,1,0:T(8,128)(2,1)}, u32[]{:S(2)}, u32[]{:S(2)}) async-start(bf16[8,2,2,128,512]{4,3,2,1,0:T(8,128)(2,1)} %get-tuple-element.72), calls=%async_computation.2 | async-start | bytes 8388608 | tf_op jit(solution)/shard_map/all_to_all | solution.py:905
  129.9 35.4 %expert_both.2 = (bf16[8,2,2,128,512]{4,3,2,1,0:T(8,128)(2,1)}, f32[512,2048]{1,0:T(8,128)}, f32[2048,512]{1,0:T(8,128)}, f32[8,2048]{1,0:T(8,128)}, f32[8,512]{1,0:T(8,128)}) custom-call(s32[8]{0:T(128)} %convert_reduce_fusion.cnt_ref, bf16[8,2,2,128,512]{4,3,2,1,0:T(8,128)(2,1)} %all-to-all-done.3.x_ref, ...), custom_call_target="tpu_custom_call" | custom-call | flops 40000000000 | bytes 20000000 | tf_op jit(solution)/shard_map/expert_both/pallas_call | solution.py:483
  165.3 12.5 %all-to-all-done.2.x_ref = bf16[8,2,2,128,512]{4,3,2,1,0:T(8,128)(2,1)} async-done(((bf16[8,2,2,128,512]{4,3,2,1,0:T(8,128)(2,1)}), bf16[8,2,2,128,512]{4,3,2,1,0:T(8,128)(2,1)}, u32[]{:S(2)}, u32[]{:S(2)}) %all-to-all-start.2) | async-done | bytes 4194336 | tf_op jit(solution)/shard_map/all_to_all | solution.py:905
  177.8 4.6 %all-to-all-start.5 = ((bf16[8,2,2,128,512]{4,3,2,1,0:T(8,128)(2,1)}), bf16[8,2,2,128,512]{4,3,2,1,0:T(8,128)(2,1)}, u32[]{:S(2)}, u32[]{:S(2)}) async-start(bf16[8,2,2,128,512]{4,3,2,1,0:T(8,128)(2,1)} %get-tuple-element.89), calls=%async_computation.5 | async-start | bytes 8388608 | tf_op jit(solution)/shard_map/all_to_all | solution.py:905
  182.4 9.9 %expert_both.3 = (bf16[8,2,2,128,512]{4,3,2,1,0:T(8,128)(2,1)}, bf16[32,128,512]{2,1,0:T(8,128)(2,1)}, f32[8,2048]{1,0:T(8,128)}, f32[8,512]{1,0:T(8,128)}) custom-call(s32[8]{0:T(128)} %convert_reduce_fusion.cnt_ref, bf16[8,2,2,128,512]{4,3,2,1,0:T(8,128)(2,1)} %all-to-all-done.2.x_ref, bf16[32,128,512]{2,1,0:T(8,128)(2,1)} %all-gather.2.cloned.1.call-done.w_ref, ...), custom_call_target="tpu_custom_call" | custom-call | flops 40000000000 | bytes 20000000 | tf_op jit(solution)/shard_map/expert_both/pallas_call | solution.py:483
  195.0 36.5 %all-to-all-done.5.y_ref = bf16[8,2,2,128,512]{4,3,2,1,0:T(8,128)(2,1)} async-done(((bf16[8,2,2,128,512]{4,3,2,1,0:T(8,128)(2,1)}), bf16[8,2,2,128,512]{4,3,2,1,0:T(8,128)(2,1)}, u32[]{:S(2)}, u32[]{:S(2)}) %all-to-all-start.5) | async-done | bytes 4194336 | tf_op jit(solution)/shard_map/all_to_all | solution.py:905
  231.5 5.0 %all-to-all-start.4 = ((bf16[8,2,2,128,512]{4,3,2,1,0:T(8,128)(2,1)}), bf16[8,2,2,128,512]{4,3,2,1,0:T(8,128)(2,1)}, u32[]{:S(2)}, u32[]{:S(2)}) async-start(bf16[8,2,2,128,512]{4,3,2,1,0:T(8,128)(2,1)} %get-tuple-element.79), calls=%async_computation.4 | async-start | bytes 8388608 | tf_op jit(solution)/shard_map/all_to_all | solution.py:905
  237.1 24.6 %dense_backward.2 = (bf16[8,197,512]{2,1,0:T(8,128)(2,1)}, bf16[8,197,512]{2,1,0:T(8,128)(2,1)}, f32[512,2048]{1,0:T(8,128)}, f32[128,512]{1,0:T(8,128)}) custom-call(s32[1]{0:T(128)} %copy.72.cnt_ref, bf16[4,197,512]{2,1,0:T(8,128)(2,1)} %copy.63.img_ref, bf16[4,197,512]{2,1,0:T(8,128)(2,1)} %copy.64.cot_ref, f32[8,8,208]{2,1,0:T(8,128)} %select_maximum_fusion.meta_ref, ...), custom_call_target="tpu_custom_call" | custom-call | flops 40000000000 | bytes 20000000 | tf_op jit(solution)/shard_map/dense_backward/pallas_call | solution.py:758
  261.6 24.0 %all-to-all-done.4.y_ref = bf16[8,2,2,128,512]{4,3,2,1,0:T(8,128)(2,1)} async-done(((bf16[8,2,2,128,512]{4,3,2,1,0:T(8,128)(2,1)}), bf16[8,2,2,128,512]{4,3,2,1,0:T(8,128)(2,1)}, u32[]{:S(2)}, u32[]{:S(2)}) %all-to-all-start.4) | async-done | bytes 4194336 | tf_op jit(solution)/shard_map/all_to_all | solution.py:905
  285.6 10.3 %dense_backward.3 = (bf16[8,197,512]{2,1,0:T(8,128)(2,1)}, bf16[8,197,512]{2,1,0:T(8,128)(2,1)}, bf16[2,16,16,2176]{3,2,1,0:T(8,128)(2,1)}) custom-call(s32[1]{0:T(128)} %copy.72.cnt_ref, bf16[4,197,512]{2,1,0:T(8,128)(2,1)} %copy.61.img_ref, bf16[4,197,512]{2,1,0:T(8,128)(2,1)} %copy.62.cot_ref, ...), custom_call_target="tpu_custom_call", output_to_operand_aliasing={{0}: (16, {}), {1}: (17, {})} | custom-call | flops 40000000000 | bytes 20000000 | tf_op jit(solution)/shard_map/dense_backward/pallas_call | solution.py:758
  295.9 6.7 %all_to_all.40 = bf16[2,16,16,2176]{3,2,1,0:T(8,128)(2,1)S(1)} all-to-all(bf16[2,16,16,2176]{3,2,1,0:T(8,128)(2,1)} %get-tuple-element.101), channel_id=1, replica_groups={{0,1},{2,3},{4,5},{6,7},{8,9},{10,11},{12,13},{14,15},{16,17},{18,19},{..., dimensions={0} | all-to-all | bytes 4456448 | tf_op jit(solution)/shard_map/all_to_all | solution.py:1157
  304.3 19.6 %all-to-all-start.7 = ((bf16[16,16,2176]{2,1,0:T(8,128)(2,1)}), bf16[16,16,2176]{2,1,0:T(8,128)(2,1)S(1)}, u32[]{:S(2)}, u32[]{:S(2)}) async-start(bf16[16,16,2176]{2,1,0:T(8,128)(2,1)} %reduce_sum.22), calls=%async_computation.7 | async-start | bytes 2228224 | tf_op jit(solution)/shard_map/all_to_all | solution.py:1159
  324.0 2.2 dynamic-slice_bitcast_fusion
  326.2 1.9 collective-permute-start.5
  328.3 1.7 collective-permute-start.7
  330.0 2.6 collective-permute-start.9
  332.6 2.3 collective-permute-start.10
  338.2 11.8 %all-to-all-done.7.got_ref = bf16[16,16,2176]{2,1,0:T(8,128)(2,1)S(1)} async-done(((bf16[16,16,2176]{2,1,0:T(8,128)(2,1)}), bf16[16,16,2176]{2,1,0:T(8,128)(2,1)S(1)}, u32[]{:S(2)}, u32[]{:S(2)}) %all-to-all-start.7) | async-done | bytes 1114144 | tf_op jit(solution)/shard_map/all_to_all | solution.py:1159
  351.3 3.2 finish.1
  (106 shorter events, 28.1 us)
Async XLA Ops:
  9.4 20.6 %all-to-all-start = ((bf16[8,128,512]{2,1,0:T(8,128)(2,1)}), bf16[8,128,512]{2,1,0:T(8,128)(2,1)S(1)}, u32[]{:S(2)}, u32[]{:S(2)}) async-start(bf16[8,128,512]{2,1,0:T(8,128)(2,1)} %pack.1), calls=%async_computation | async-start | bytes 2097152 | tf_op jit(solution)/shard_map/all_to_all | solution.py:905
  14.6 20.9 %copy-start.4 = (bf16[8,197,512]{2,0,1:T(8,128)(2,1)S(1)}, bf16[8,197,512]{2,0,1:T(8,128)(2,1)}, u32[]{:S(2)}) copy-start(bf16[8,197,512]{2,0,1:T(8,128)(2,1)} %param.19) | copy-start | bytes 4841476
  17.1 7.0 %collective-permute-start.2 = (bf16[16,2176]{1,0:T(8,128)(2,1)}, bf16[16,2176]{1,0:T(8,128)(2,1)S(1)}, u32[]{:S(2)}, u32[]{:S(2)}) collective-permute-start(bf16[16,2176]{1,0:T(8,128)(2,1)} %prepare.1), channel_id=1, source_target_pairs={{0,24},{1,25},{2,26},{3,27},{4,28},{5,29},{6,30},{7,31},{8,16},{9,... | collective-permute-start | bytes 208904 | tf_op jit(solution)/shard_map/ppermute | solution.py:973
  20.7 6.7 %collective-permute-start.1 = (bf16[16,2176]{1,0:T(8,128)(2,1)}, bf16[16,2176]{1,0:T(8,128)(2,1)S(1)}, u32[]{:S(2)}, u32[]{:S(2)}) collective-permute-start(bf16[16,2176]{1,0:T(8,128)(2,1)} %prepare.1), channel_id=1, source_target_pairs={{0,16},{1,17},{2,18},{3,19},{4,20},{5,21},{6,22},{7,23},{8,24},{9,... | collective-permute-start | bytes 208904 | tf_op jit(solution)/shard_map/ppermute | solution.py:973
  20.7 6.7 %collective-permute-start = (bf16[16,2176]{1,0:T(8,128)(2,1)}, bf16[16,2176]{1,0:T(8,128)(2,1)S(1)}, u32[]{:S(2)}, u32[]{:S(2)}) collective-permute-start(bf16[16,2176]{1,0:T(8,128)(2,1)} %prepare.1), channel_id=1, source_target_pairs={{0,8},{1,9},{2,10},{3,11},{4,12},{5,13},{6,14},{7,15},{8,0},{9,1},... | collective-permute-start | bytes 208904 | tf_op jit(solution)/shard_map/ppermute | solution.py:973
  30.0 6.1 %copy-start.1 = (bf16[8,128,512]{2,1,0:T(8,128)(2,1)}, bf16[8,128,512]{2,1,0:T(8,128)(2,1)S(1)}, u32[]{:S(2)}) copy-start(bf16[8,128,512]{2,1,0:T(8,128)(2,1)S(1)} %all-to-all-done) | copy-start | bytes 3145732
  31.2 18.0 %all-to-all-start.1 = ((bf16[4,64,2176]{2,1,0:T(8,128)(2,1)}), bf16[4,64,2176]{2,1,0:T(8,128)(2,1)}, u32[]{:S(2)}, u32[]{:S(2)}) async-start(bf16[4,64,2176]{2,1,0:T(8,128)(2,1)} %broadcast_in_dim.82), calls=%async_computation.1 | async-start | bytes 2228224 | tf_op jit(solution)/shard_map/all_to_all | solution.py:986
  35.5 93.2 %all-gather.2.cloned.1.call-start = ((), (), s32[]{:S(2)}) async-start(), calls=%async_computation.9 | async-start | bytes 5242880 | tf_op jit(solution)/shard_map/all_gather | solution.py:911
  35.5 1.6 copy-start.5
  37.1 12.0 %copy-start.6 = (s32[8,197,2]{1,2,0:T(2,128)S(1)}, s32[8,197,2]{1,2,0:T(2,128)}, u32[]{:S(2)}) copy-start(s32[8,197,2]{1,2,0:T(2,128)} %param.21) | copy-start | bytes 37828
  37.1 12.0 %copy-start.11 = (s32[8,197,2]{1,2,0:T(2,128)S(1)}, s32[8,197,2]{1,2,0:T(2,128)}, u32[]{:S(2)}) copy-start(s32[8,197,2]{1,2,0:T(2,128)} %param.23) | copy-start | bytes 37828
  37.1 12.1 %copy-start.12 = (s32[8,197,2]{1,2,0:T(2,128)S(1)}, s32[8,197,2]{1,2,0:T(2,128)}, u32[]{:S(2)}) copy-start(s32[8,197,2]{1,2,0:T(2,128)} %param.22) | copy-start | bytes 37828
  49.1 3.0 collective-permute-start.3
  69.9 54.2 %all-to-all-start.3 = ((bf16[8,2,2,128,512]{4,3,2,1,0:T(8,128)(2,1)}), bf16[8,2,2,128,512]{4,3,2,1,0:T(8,128)(2,1)}, u32[]{:S(2)}, u32[]{:S(2)}) async-start(bf16[8,2,2,128,512]{4,3,2,1,0:T(8,128)(2,1)} %get-tuple-element.74), calls=%async_computation.3 | async-start | bytes 8388608 | tf_op jit(solution)/shard_map/all_to_all | solution.py:905
  124.1 53.7 %all-to-all-start.2 = ((bf16[8,2,2,128,512]{4,3,2,1,0:T(8,128)(2,1)}), bf16[8,2,2,128,512]{4,3,2,1,0:T(8,128)(2,1)}, u32[]{:S(2)}, u32[]{:S(2)}) async-start(bf16[8,2,2,128,512]{4,3,2,1,0:T(8,128)(2,1)} %get-tuple-element.72), calls=%async_computation.2 | async-start | bytes 8388608 | tf_op jit(solution)/shard_map/all_to_all | solution.py:905
  177.8 53.7 %all-to-all-start.5 = ((bf16[8,2,2,128,512]{4,3,2,1,0:T(8,128)(2,1)}), bf16[8,2,2,128,512]{4,3,2,1,0:T(8,128)(2,1)}, u32[]{:S(2)}, u32[]{:S(2)}) async-start(bf16[8,2,2,128,512]{4,3,2,1,0:T(8,128)(2,1)} %get-tuple-element.89), calls=%async_computation.5 | async-start | bytes 8388608 | tf_op jit(solution)/shard_map/all_to_all | solution.py:905
  182.4 141.6 %reduce-scatter.2.cloned.1.call-start = ((), (), s32[]{:S(2)}) async-start(), calls=%async_computation.10 | async-start | bytes 5242880 | tf_op jit(solution)/shard_map/reduce_scatter | solution.py:1089
  194.3 37.2 %copy-start.13 = (f32[128,512]{1,0:T(8,128)}, f32[128,512]{1,0:T(8,128)S(1)}, u32[]{:S(2)}) copy-start(f32[128,512]{1,0:T(8,128)S(1)} %broadcast_dynamic-update-slice_fusion.extra_ref) | copy-start | bytes 786436
  231.5 54.1 %all-to-all-start.4 = ((bf16[8,2,2,128,512]{4,3,2,1,0:T(8,128)(2,1)}), bf16[8,2,2,128,512]{4,3,2,1,0:T(8,128)(2,1)}, u32[]{:S(2)}, u32[]{:S(2)}) async-start(bf16[8,2,2,128,512]{4,3,2,1,0:T(8,128)(2,1)} %get-tuple-element.79), calls=%async_computation.4 | async-start | bytes 8388608 | tf_op jit(solution)/shard_map/all_to_all | solution.py:905
  304.3 30.5 %copy-start.2 = (bf16[8,197,512]{2,1,0:T(8,128)(2,1)S(1)}, bf16[8,197,512]{2,1,0:T(8,128)(2,1)}, u32[]{:S(2)}) copy-start(bf16[8,197,512]{2,1,0:T(8,128)(2,1)} %get-tuple-element.150) | copy-start | bytes 4841476
  304.3 45.6 %all-to-all-start.7 = ((bf16[16,16,2176]{2,1,0:T(8,128)(2,1)}), bf16[16,16,2176]{2,1,0:T(8,128)(2,1)S(1)}, u32[]{:S(2)}, u32[]{:S(2)}) async-start(bf16[16,16,2176]{2,1,0:T(8,128)(2,1)} %reduce_sum.22), calls=%async_computation.7 | async-start | bytes 2228224 | tf_op jit(solution)/shard_map/all_to_all | solution.py:1159
  324.0 12.5 %copy-start.3 = (bf16[8,197,512]{2,1,0:T(8,128)(2,1)S(1)}, bf16[8,197,512]{2,1,0:T(8,128)(2,1)}, u32[]{:S(2)}) copy-start(bf16[8,197,512]{2,1,0:T(8,128)(2,1)} %get-tuple-element.151) | copy-start | bytes 4841476
  326.2 3.7 %collective-permute-start.4 = (bf16[128,512]{1,0:T(8,128)(2,1)S(1)}, bf16[128,512]{1,0:T(8,128)(2,1)S(1)}, u32[]{:S(2)}, u32[]{:S(2)}) collective-permute-start(bf16[128,512]{1,0:T(8,128)(2,1)S(1)} %get-tuple-element.176), channel_id=1, source_target_pairs={{0,1},{1,0},{2,3},{3,2},{4,5},{5,4},{6,7},{7,6},{8,9},{9,8},{10,11... | collective-permute-start | bytes 393224 | tf_op jit(solution)/shard_map/ppermute | solution.py:1098
  326.2 6.3 %collective-permute-start.5 = (bf16[128,512]{1,0:T(8,128)(2,1)S(1)}, bf16[128,512]{1,0:T(8,128)(2,1)S(1)}, u32[]{:S(2)}, u32[]{:S(2)}) collective-permute-start(bf16[128,512]{1,0:T(8,128)(2,1)S(1)} %get-tuple-element.175), channel_id=1, source_target_pairs={{0,2},{1,3},{2,0},{3,1},{4,6},{5,7},{6,4},{7,5},{8,10},{9,11},{10,... | collective-permute-start | bytes 393224 | tf_op jit(solution)/shard_map/ppermute | solution.py:1098
  328.2 21.8 %collective-permute-start.6 = (bf16[128,512]{1,0:T(8,128)(2,1)}, bf16[128,512]{1,0:T(8,128)(2,1)S(1)}, u32[]{:S(2)}, u32[]{:S(2)}) collective-permute-start(bf16[128,512]{1,0:T(8,128)(2,1)} %get-tuple-element.174), channel_id=1, source_target_pairs={{0,3},{1,2},{2,1},{3,0},{4,7},{5,6},{6,5},{7,4},{8,11},{9,10},{10,... | collective-permute-start | bytes 393224 | tf_op jit(solution)/shard_map/ppermute | solution.py:1098
  328.3 21.7 %collective-permute-start.7 = (bf16[128,512]{1,0:T(8,128)(2,1)}, bf16[128,512]{1,0:T(8,128)(2,1)S(1)}, u32[]{:S(2)}, u32[]{:S(2)}) collective-permute-start(bf16[128,512]{1,0:T(8,128)(2,1)} %get-tuple-element.173), channel_id=1, source_target_pairs={{0,4},{1,5},{2,6},{3,7},{4,0},{5,1},{6,2},{7,3},{8,12},{9,13},{10,... | collective-permute-start | bytes 393224 | tf_op jit(solution)/shard_map/ppermute | solution.py:1098
  330.0 20.0 %collective-permute-start.8 = (bf16[128,512]{1,0:T(8,128)(2,1)}, bf16[128,512]{1,0:T(8,128)(2,1)}, u32[]{:S(2)}, u32[]{:S(2)}) collective-permute-start(bf16[128,512]{1,0:T(8,128)(2,1)} %get-tuple-element.172), channel_id=1, source_target_pairs={{0,5},{1,4},{2,7},{3,6},{4,1},{5,0},{6,3},{7,2},{8,13},{9,12},{10,... | collective-permute-start | bytes 393224 | tf_op jit(solution)/shard_map/ppermute | solution.py:1098
  330.0 8.2 %copy-start.7 = (bf16[128,512]{1,0:T(8,128)(2,1)}, bf16[128,512]{1,0:T(8,128)(2,1)S(1)}, u32[]{:S(2)}) copy-start(bf16[128,512]{1,0:T(8,128)(2,1)S(1)} %collective-permute-done.4.refs_1_) | copy-start | bytes 393220
  330.0 20.0 %collective-permute-start.9 = (bf16[128,512]{1,0:T(8,128)(2,1)S(1)}, bf16[128,512]{1,0:T(8,128)(2,1)}, u32[]{:S(2)}, u32[]{:S(2)}) collective-permute-start(bf16[128,512]{1,0:T(8,128)(2,1)S(1)} %get-tuple-element.171), channel_id=1, source_target_pairs={{0,6},{1,7},{2,4},{3,5},{4,2},{5,3},{6,0},{7,1},{8,14},{9,15},{10,... | collective-permute-start | bytes 393224 | tf_op jit(solution)/shard_map/ppermute | solution.py:1098
  332.6 5.6 %copy-start.8 = (bf16[128,512]{1,0:T(8,128)(2,1)}, bf16[128,512]{1,0:T(8,128)(2,1)S(1)}, u32[]{:S(2)}) copy-start(bf16[128,512]{1,0:T(8,128)(2,1)S(1)} %collective-permute-done.5.refs_2_) | copy-start | bytes 393220
  332.6 18.8 %collective-permute-start.10 = (bf16[128,512]{1,0:T(8,128)(2,1)S(1)}, bf16[128,512]{1,0:T(8,128)(2,1)}, u32[]{:S(2)}, u32[]{:S(2)}) collective-permute-start(bf16[128,512]{1,0:T(8,128)(2,1)S(1)} %get-tuple-element.170), channel_id=1, source_target_pairs={{0,7},{1,6},{2,5},{3,4},{4,3},{5,2},{6,1},{7,0},{8,15},{9,14},{10,... | collective-permute-start | bytes 393224 | tf_op jit(solution)/shard_map/ppermute | solution.py:1098
  350.0 1.4 copy-start
  (3 other events, 3.7 us)
Sparse Core Ops, SparseCore 0:
  38.9 82.3 all-gather.1
  195.1 96.0 reduce-scatter.1
where the time goes:
time: 366 us; the launch traced here: 362 us
  waiting for transfers between devices  139 us (38%)
  Pallas kernels  111 us (30%)
  starting transfers between devices  61.3 us (17%)
  local copies, waits for them, and re-layouts  20.2 us (6%)
  between operations  17.3 us (5%)
  blocking collectives  6.74 us (2%)
  other arithmetic  6.01 us (2%)
    all_to_all x5, waiting for transfers between devices, plane_swap(): lax.all_to_all(v, 'dp', 0, 0, tiled=True, axis_index_groups=plane_groups)  108 us
    pallas_call x2, Pallas kernels, expert_call(): pl.pallas_call(functools.partial(expert_kernel, m0, mbc, acc is not None,...  45.3 us
    pallas_call x2, Pallas kernels, backward_call(): pl.pallas_call(functools.partial(backward_kernel, m0, seq_len, pad_len, a...  34.8 us
    all_to_all x5, starting transfers between devices, plane_swap(): lax.all_to_all(v, 'dp', 0, 0, tiled=True, axis_index_groups=plane_groups)  24.3 us
    pallas_call x2, Pallas kernels, forward_call(): pl.pallas_call(functools.partial(forward_kernel, m0, seq_len, pad_len, as...  23.8 us
    all_to_all x1, starting transfers between devices, shards(): lax.all_to_all(grads.reshape(total // CORES, rows, wide), 'dp', 0, 0, til...  19.6 us
    all_to_all x1, waiting for transfers between devices, shards(): lax.all_to_all(grads.reshape(total // CORES, rows, wide), 'dp', 0, 0, til...  11.8 us
    all_to_all x1, waiting for transfers between devices, shards(): lax.all_to_all(packed, 'dp', 0, 0, tiled=True, axis_index_groups=core_gro...  10.3 us
  transfers between devices with their start and end apart: 20, of which 11 were waited for; matrix products, arithmetic and copies ran while one was open for 7% of the time, Pallas kernels for 29%

commit v1 on v0

--- a/solution.py
+++ b/solution.py
@@ -799,7 +799,7 @@
         in_ref, back_ref = refs[:2]
         half, wide_of = back_ref.shape[1:]
         for r, block in enumerate(experts):
-            e = lax.bitwise_xor(lax.rem(lax.axis_index("dp"), EXPERTS), r)
+            e = lax.bitwise_xor(lax.rem(lax.axis_index("dp"), EXPERTS), count - 1 - r)
             for c in range(half // BLOCK):
                 in_ref[e, :, c * wide_of : (c + 1) * wide_of] = block[
                     c * BLOCK : (c + 1) * BLOCK, :
@@ -1091,12 +1091,13 @@
     )
     if rows == BLOCK:
         place = me % EXPERTS
-        blocks_in = []
-        for r in range(EXPERTS):
+        blocks_in = {}
+        for r in reversed(range(EXPERTS)):
             block = lax.dynamic_index_in_dim(expert_grads, place ^ r, 0, keepdims=False)
             if r:
                 block = lax.ppermute(block, "dp", [(i, i ^ r) for i in range(total)])
-            blocks_in.append(block)
+            blocks_in[r] = block
+        blocks_in = [blocks_in[r] for r in reversed(range(EXPERTS))]
     else:
         blocks_in = []
         expert_grads = plane_swap(expert_grads).astype(F32)

time: 366 us -> 370 us (1.011)
    ppermute x7, waiting for transfers between devices: 1.33 us -> 11.5 us  [shards(): block = lax.ppermute(block, 'dp', [(i, i ^ r) for i in range(total)])]
    all_to_all x1, waiting for transfers between devices: 11.8 us -> 3.28 us  [shards(): lax.all_to_all(grads.reshape(total // CORES, rows, wide), 'dp', 0, 0, til...]
  transfers between devices with their start and end apart: 20 -> 20, of which waited for: 11 -> 13; matrix products, arithmetic and copies ran while one was open for 7% -> 7% of each run, Pallas kernels for 29% -> 29%
where the time goes in v1:
time: 370 us; the launch traced here: 362 us
  waiting for transfers between devices  141 us (38%)
  Pallas kernels  111 us (30%)
  starting transfers between devices  60.2 us (16%)
  local copies, waits for them, and re-layouts  20.2 us (5%)
  between operations  17.3 us (5%)
  blocking collectives  6.74 us (2%)
  other arithmetic  6.01 us (2%)
    all_to_all x5, waiting for transfers between devices, plane_swap(): lax.all_to_all(v, 'dp', 0, 0, tiled=True, axis_index_groups=plane_groups)  108 us
    pallas_call x2, Pallas kernels, expert_call(): pl.pallas_call(functools.partial(expert_kernel, m0, mbc, acc is not None,...  45.3 us
    pallas_call x2, Pallas kernels, backward_call(): pl.pallas_call(functools.partial(backward_kernel, m0, seq_len, pad_len, a...  34.8 us
    all_to_all x5, starting transfers between devices, plane_swap(): lax.all_to_all(v, 'dp', 0, 0, tiled=True, axis_index_groups=plane_groups)  24.3 us
    pallas_call x2, Pallas kernels, forward_call(): pl.pallas_call(functools.partial(forward_kernel, m0, seq_len, pad_len, as...  23.8 us
    all_to_all x1, starting transfers between devices, shards(): lax.all_to_all(grads.reshape(total // CORES, rows, wide), 'dp', 0, 0, til...  19.6 us
    ppermute x7, waiting for transfers between devices, shards(): block = lax.ppermute(block, 'dp', [(i, i ^ r) for i in range(total)])  11.5 us
    all_to_all x1, waiting for transfers between devices, shards(): lax.all_to_all(packed, 'dp', 0, 0, tiled=True, axis_index_groups=core_gro...  10.3 us
  transfers between devices with their start and end apart: 20, of which 13 were waited for; matrix products, arithmetic and copies ran while one was open for 7% of the time, Pallas kernels for 29%

profile of v1, /device:TPU:0, one launch (start us, length us, event | category | flops | bytes accessed | tf_op | source)
XLA Modules:
  0.0 362.2 jit_solution(13410560212041554255)
XLA Ops:
  7.2 2.2 pack.1
  9.4 5.2 %all-to-all-start = ((bf16[8,128,512]{2,1,0:T(8,128)(2,1)}), bf16[8,128,512]{2,1,0:T(8,128)(2,1)S(1)}, u32[]{:S(2)}, u32[]{:S(2)}) async-start(bf16[8,128,512]{2,1,0:T(8,128)(2,1)} %pack.1), calls=%async_computation | async-start | bytes 2097152 | tf_op jit(solution)/shard_map/all_to_all | solution.py:905
  17.1 3.6 collective-permute-start.2
  21.5 2.6 collective-permute-done.2
  24.0 3.3 collective-permute-done.1
  31.2 4.3 %all-to-all-start.1 = ((bf16[4,64,2176]{2,1,0:T(8,128)(2,1)}), bf16[4,64,2176]{2,1,0:T(8,128)(2,1)}, u32[]{:S(2)}, u32[]{:S(2)}) async-start(bf16[4,64,2176]{2,1,0:T(8,128)(2,1)} %broadcast_in_dim.82), calls=%async_computation.1 | async-start | bytes 2228224 | tf_op jit(solution)/shard_map/all_to_all | solution.py:986
  38.8 10.3 %all-to-all-done.1.first_ref = bf16[4,64,2176]{2,1,0:T(8,128)(2,1)} async-done(((bf16[4,64,2176]{2,1,0:T(8,128)(2,1)}), bf16[4,64,2176]{2,1,0:T(8,128)(2,1)}, u32[]{:S(2)}, u32[]{:S(2)}) %all-to-all-start.1) | async-done | bytes 1114144 | tf_op jit(solution)/shard_map/all_to_all | solution.py:986
  50.0 2.1 collective-permute-done.3.second_ref
  53.1 16.8 %dense_forward.2 = (bf16[8,2,2,128,512]{4,3,2,1,0:T(8,128)(2,1)}, bf16[2,416,1536]{2,1,0:T(8,128)(2,1)}, bf16[2,2,4,416,208]{4,3,2,1,0:T(8,128)(2,1)}, bf16[2,41...) custom-call(s32[1]{0:T(128)} %copy.72.cnt_ref, ...), custom_call_target="tpu_custom_call" | custom-call | flops 16000000000 | bytes 20000000 | tf_op jit(solution)/shard_map/dense_forward/pallas_call | solution.py:314
  69.9 5.1 %all-to-all-start.3 = ((bf16[8,2,2,128,512]{4,3,2,1,0:T(8,128)(2,1)}), bf16[8,2,2,128,512]{4,3,2,1,0:T(8,128)(2,1)}, u32[]{:S(2)}, u32[]{:S(2)}) async-start(bf16[8,2,2,128,512]{4,3,2,1,0:T(8,128)(2,1)} %get-tuple-element.74), calls=%async_computation.3 | async-start | bytes 8388608 | tf_op jit(solution)/shard_map/all_to_all | solution.py:905
  82.7 7.0 %dense_forward.3 = (bf16[8,2,2,128,512]{4,3,2,1,0:T(8,128)(2,1)}, bf16[2,416,1536]{2,1,0:T(8,128)(2,1)}, bf16[2,2,4,416,208]{4,3,2,1,0:T(8,128)(2,1)}, bf16[2,41...) custom-call(s32[1]{0:T(128)} %copy.72.cnt_ref, ...), custom_call_target="tpu_custom_call" | custom-call | flops 16000000000 | bytes 20000000 | tf_op jit(solution)/shard_map/dense_forward/pallas_call | solution.py:314
  91.2 32.8 %all-to-all-done.3.x_ref = bf16[8,2,2,128,512]{4,3,2,1,0:T(8,128)(2,1)} async-done(((bf16[8,2,2,128,512]{4,3,2,1,0:T(8,128)(2,1)}), bf16[8,2,2,128,512]{4,3,2,1,0:T(8,128)(2,1)}, u32[]{:S(2)}, u32[]{:S(2)}) %all-to-all-start.3) | async-done | bytes 4194336 | tf_op jit(solution)/shard_map/all_to_all | solution.py:905
  124.1 4.6 %all-to-all-start.2 = ((bf16[8,2,2,128,512]{4,3,2,1,0:T(8,128)(2,1)}), bf16[8,2,2,128,512]{4,3,2,1,0:T(8,128)(2,1)}, u32[]{:S(2)}, u32[]{:S(2)}) async-start(bf16[8,2,2,128,512]{4,3,2,1,0:T(8,128)(2,1)} %get-tuple-element.72), calls=%async_computation.2 | async-start | bytes 8388608 | tf_op jit(solution)/shard_map/all_to_all | solution.py:905
  129.9 35.4 %expert_both.2 = (bf16[8,2,2,128,512]{4,3,2,1,0:T(8,128)(2,1)}, f32[512,2048]{1,0:T(8,128)}, f32[2048,512]{1,0:T(8,128)}, f32[8,2048]{1,0:T(8,128)}, f32[8,512]{1,0:T(8,128)}) custom-call(s32[8]{0:T(128)} %convert_reduce_fusion.cnt_ref, bf16[8,2,2,128,512]{4,3,2,1,0:T(8,128)(2,1)} %all-to-all-done.3.x_ref, ...), custom_call_target="tpu_custom_call" | custom-call | flops 40000000000 | bytes 20000000 | tf_op jit(solution)/shard_map/expert_both/pallas_call | solution.py:483
  165.3 12.5 %all-to-all-done.2.x_ref = bf16[8,2,2,128,512]{4,3,2,1,0:T(8,128)(2,1)} async-done(((bf16[8,2,2,128,512]{4,3,2,1,0:T(8,128)(2,1)}), bf16[8,2,2,128,512]{4,3,2,1,0:T(8,128)(2,1)}, u32[]{:S(2)}, u32[]{:S(2)}) %all-to-all-start.2) | async-done | bytes 4194336 | tf_op jit(solution)/shard_map/all_to_all | solution.py:905
  177.8 4.6 %all-to-all-start.5 = ((bf16[8,2,2,128,512]{4,3,2,1,0:T(8,128)(2,1)}), bf16[8,2,2,128,512]{4,3,2,1,0:T(8,128)(2,1)}, u32[]{:S(2)}, u32[]{:S(2)}) async-start(bf16[8,2,2,128,512]{4,3,2,1,0:T(8,128)(2,1)} %get-tuple-element.89), calls=%async_computation.5 | async-start | bytes 8388608 | tf_op jit(solution)/shard_map/all_to_all | solution.py:905
  182.4 9.9 %expert_both.3 = (bf16[8,2,2,128,512]{4,3,2,1,0:T(8,128)(2,1)}, bf16[32,128,512]{2,1,0:T(8,128)(2,1)}, f32[8,2048]{1,0:T(8,128)}, f32[8,512]{1,0:T(8,128)}) custom-call(s32[8]{0:T(128)} %convert_reduce_fusion.cnt_ref, bf16[8,2,2,128,512]{4,3,2,1,0:T(8,128)(2,1)} %all-to-all-done.2.x_ref, bf16[32,128,512]{2,1,0:T(8,128)(2,1)} %all-gather.2.cloned.1.call-done.w_ref, ...), custom_call_target="tpu_custom_call" | custom-call | flops 40000000000 | bytes 20000000 | tf_op jit(solution)/shard_map/expert_both/pallas_call | solution.py:483
  195.0 36.5 %all-to-all-done.5.y_ref = bf16[8,2,2,128,512]{4,3,2,1,0:T(8,128)(2,1)} async-done(((bf16[8,2,2,128,512]{4,3,2,1,0:T(8,128)(2,1)}), bf16[8,2,2,128,512]{4,3,2,1,0:T(8,128)(2,1)}, u32[]{:S(2)}, u32[]{:S(2)}) %all-to-all-start.5) | async-done | bytes 4194336 | tf_op jit(solution)/shard_map/all_to_all | solution.py:905
  231.5 5.0 %all-to-all-start.4 = ((bf16[8,2,2,128,512]{4,3,2,1,0:T(8,128)(2,1)}), bf16[8,2,2,128,512]{4,3,2,1,0:T(8,128)(2,1)}, u32[]{:S(2)}, u32[]{:S(2)}) async-start(bf16[8,2,2,128,512]{4,3,2,1,0:T(8,128)(2,1)} %get-tuple-element.79), calls=%async_computation.4 | async-start | bytes 8388608 | tf_op jit(solution)/shard_map/all_to_all | solution.py:905
  237.1 24.6 %dense_backward.2 = (bf16[8,197,512]{2,1,0:T(8,128)(2,1)}, bf16[8,197,512]{2,1,0:T(8,128)(2,1)}, f32[512,2048]{1,0:T(8,128)}, f32[128,512]{1,0:T(8,128)}) custom-call(s32[1]{0:T(128)} %copy.72.cnt_ref, bf16[4,197,512]{2,1,0:T(8,128)(2,1)} %copy.63.img_ref, bf16[4,197,512]{2,1,0:T(8,128)(2,1)} %copy.64.cot_ref, f32[8,8,208]{2,1,0:T(8,128)} %select_maximum_fusion.meta_ref, ...), custom_call_target="tpu_custom_call" | custom-call | flops 40000000000 | bytes 20000000 | tf_op jit(solution)/shard_map/dense_backward/pallas_call | solution.py:758
  261.6 24.0 %all-to-all-done.4.y_ref = bf16[8,2,2,128,512]{4,3,2,1,0:T(8,128)(2,1)} async-done(((bf16[8,2,2,128,512]{4,3,2,1,0:T(8,128)(2,1)}), bf16[8,2,2,128,512]{4,3,2,1,0:T(8,128)(2,1)}, u32[]{:S(2)}, u32[]{:S(2)}) %all-to-all-start.4) | async-done | bytes 4194336 | tf_op jit(solution)/shard_map/all_to_all | solution.py:905
  285.6 10.3 %dense_backward.3 = (bf16[8,197,512]{2,1,0:T(8,128)(2,1)}, bf16[8,197,512]{2,1,0:T(8,128)(2,1)}, bf16[2,16,16,2176]{3,2,1,0:T(8,128)(2,1)}) custom-call(s32[1]{0:T(128)} %copy.72.cnt_ref, bf16[4,197,512]{2,1,0:T(8,128)(2,1)} %copy.61.img_ref, bf16[4,197,512]{2,1,0:T(8,128)(2,1)} %copy.62.cot_ref, ...), custom_call_target="tpu_custom_call", output_to_operand_aliasing={{0}: (16, {}), {1}: (17, {})} | custom-call | flops 40000000000 | bytes 20000000 | tf_op jit(solution)/shard_map/dense_backward/pallas_call | solution.py:758
  295.9 6.7 %all_to_all.40 = bf16[2,16,16,2176]{3,2,1,0:T(8,128)(2,1)S(1)} all-to-all(bf16[2,16,16,2176]{3,2,1,0:T(8,128)(2,1)} %get-tuple-element.101), channel_id=1, replica_groups={{0,1},{2,3},{4,5},{6,7},{8,9},{10,11},{12,13},{14,15},{16,17},{18,19},{..., dimensions={0} | all-to-all | bytes 4456448 | tf_op jit(solution)/shard_map/all_to_all | solution.py:1158
  304.3 19.6 %all-to-all-start.7 = ((bf16[16,16,2176]{2,1,0:T(8,128)(2,1)}), bf16[16,16,2176]{2,1,0:T(8,128)(2,1)S(1)}, u32[]{:S(2)}, u32[]{:S(2)}) async-start(bf16[16,16,2176]{2,1,0:T(8,128)(2,1)} %reduce_sum.22), calls=%async_computation.7 | async-start | bytes 2228224 | tf_op jit(solution)/shard_map/all_to_all | solution.py:1160
  324.0 2.2 dynamic-slice_bitcast_fusion
  326.2 2.0 collective-permute-start.4
  331.7 3.1 collective-permute-done.4.refs_0_
  334.7 2.1 collective-permute-start.9
  336.8 6.3 %collective-permute-done.5.refs_1_ = bf16[128,512]{1,0:T(8,128)(2,1)S(1)} collective-permute-done((bf16[128,512]{1,0:T(8,128)(2,1)S(1)}, bf16[128,512]{1,0:T(8,128)(2,1)S(1)}, u32[]{:S(2)}, u32[]{:S(2)}) %collective-permute-start.5) | collective-permute-done | bytes 131104 | tf_op jit(solution)/shard_map/ppermute | solution.py:1098
  346.5 3.3 all-to-all-done.7.got_ref
  349.8 2.1 collective-permute-done.9.refs_5_
  351.9 3.2 finish.1
  (106 shorter events, 31.9 us)
Async XLA Ops:
  9.4 20.6 %all-to-all-start = ((bf16[8,128,512]{2,1,0:T(8,128)(2,1)}), bf16[8,128,512]{2,1,0:T(8,128)(2,1)S(1)}, u32[]{:S(2)}, u32[]{:S(2)}) async-start(bf16[8,128,512]{2,1,0:T(8,128)(2,1)} %pack.1), calls=%async_computation | async-start | bytes 2097152 | tf_op jit(solution)/shard_map/all_to_all | solution.py:905
  14.6 20.9 %copy-start.4 = (bf16[8,197,512]{2,0,1:T(8,128)(2,1)S(1)}, bf16[8,197,512]{2,0,1:T(8,128)(2,1)}, u32[]{:S(2)}) copy-start(bf16[8,197,512]{2,0,1:T(8,128)(2,1)} %param.19) | copy-start | bytes 4841476
  17.1 7.0 %collective-permute-start.2 = (bf16[16,2176]{1,0:T(8,128)(2,1)}, bf16[16,2176]{1,0:T(8,128)(2,1)S(1)}, u32[]{:S(2)}, u32[]{:S(2)}) collective-permute-start(bf16[16,2176]{1,0:T(8,128)(2,1)} %prepare.1), channel_id=1, source_target_pairs={{0,24},{1,25},{2,26},{3,27},{4,28},{5,29},{6,30},{7,31},{8,16},{9,... | collective-permute-start | bytes 208904 | tf_op jit(solution)/shard_map/ppermute | solution.py:973
  20.7 6.7 %collective-permute-start.1 = (bf16[16,2176]{1,0:T(8,128)(2,1)}, bf16[16,2176]{1,0:T(8,128)(2,1)S(1)}, u32[]{:S(2)}, u32[]{:S(2)}) collective-permute-start(bf16[16,2176]{1,0:T(8,128)(2,1)} %prepare.1), channel_id=1, source_target_pairs={{0,16},{1,17},{2,18},{3,19},{4,20},{5,21},{6,22},{7,23},{8,24},{9,... | collective-permute-start | bytes 208904 | tf_op jit(solution)/shard_map/ppermute | solution.py:973
  20.7 6.7 %collective-permute-start = (bf16[16,2176]{1,0:T(8,128)(2,1)}, bf16[16,2176]{1,0:T(8,128)(2,1)S(1)}, u32[]{:S(2)}, u32[]{:S(2)}) collective-permute-start(bf16[16,2176]{1,0:T(8,128)(2,1)} %prepare.1), channel_id=1, source_target_pairs={{0,8},{1,9},{2,10},{3,11},{4,12},{5,13},{6,14},{7,15},{8,0},{9,1},... | collective-permute-start | bytes 208904 | tf_op jit(solution)/shard_map/ppermute | solution.py:973
  30.0 6.1 %copy-start.1 = (bf16[8,128,512]{2,1,0:T(8,128)(2,1)}, bf16[8,128,512]{2,1,0:T(8,128)(2,1)S(1)}, u32[]{:S(2)}) copy-start(bf16[8,128,512]{2,1,0:T(8,128)(2,1)S(1)} %all-to-all-done) | copy-start | bytes 3145732
  31.2 18.0 %all-to-all-start.1 = ((bf16[4,64,2176]{2,1,0:T(8,128)(2,1)}), bf16[4,64,2176]{2,1,0:T(8,128)(2,1)}, u32[]{:S(2)}, u32[]{:S(2)}) async-start(bf16[4,64,2176]{2,1,0:T(8,128)(2,1)} %broadcast_in_dim.82), calls=%async_computation.1 | async-start | bytes 2228224 | tf_op jit(solution)/shard_map/all_to_all | solution.py:986
  35.5 93.2 %all-gather.2.cloned.1.call-start = ((), (), s32[]{:S(2)}) async-start(), calls=%async_computation.9 | async-start | bytes 5242880 | tf_op jit(solution)/shard_map/all_gather | solution.py:911
  37.1 12.0 %copy-start.6 = (s32[8,197,2]{1,2,0:T(2,128)S(1)}, s32[8,197,2]{1,2,0:T(2,128)}, u32[]{:S(2)}) copy-start(s32[8,197,2]{1,2,0:T(2,128)} %param.21) | copy-start | bytes 37828
  37.1 12.0 %copy-start.11 = (s32[8,197,2]{1,2,0:T(2,128)S(1)}, s32[8,197,2]{1,2,0:T(2,128)}, u32[]{:S(2)}) copy-start(s32[8,197,2]{1,2,0:T(2,128)} %param.23) | copy-start | bytes 37828
  37.1 12.1 %copy-start.12 = (s32[8,197,2]{1,2,0:T(2,128)S(1)}, s32[8,197,2]{1,2,0:T(2,128)}, u32[]{:S(2)}) copy-start(s32[8,197,2]{1,2,0:T(2,128)} %param.22) | copy-start | bytes 37828
  49.1 3.0 collective-permute-start.3
  69.9 54.2 %all-to-all-start.3 = ((bf16[8,2,2,128,512]{4,3,2,1,0:T(8,128)(2,1)}), bf16[8,2,2,128,512]{4,3,2,1,0:T(8,128)(2,1)}, u32[]{:S(2)}, u32[]{:S(2)}) async-start(bf16[8,2,2,128,512]{4,3,2,1,0:T(8,128)(2,1)} %get-tuple-element.74), calls=%async_computation.3 | async-start | bytes 8388608 | tf_op jit(solution)/shard_map/all_to_all | solution.py:905
  124.1 53.7 %all-to-all-start.2 = ((bf16[8,2,2,128,512]{4,3,2,1,0:T(8,128)(2,1)}), bf16[8,2,2,128,512]{4,3,2,1,0:T(8,128)(2,1)}, u32[]{:S(2)}, u32[]{:S(2)}) async-start(bf16[8,2,2,128,512]{4,3,2,1,0:T(8,128)(2,1)} %get-tuple-element.72), calls=%async_computation.2 | async-start | bytes 8388608 | tf_op jit(solution)/shard_map/all_to_all | solution.py:905
  177.8 53.7 %all-to-all-start.5 = ((bf16[8,2,2,128,512]{4,3,2,1,0:T(8,128)(2,1)}), bf16[8,2,2,128,512]{4,3,2,1,0:T(8,128)(2,1)}, u32[]{:S(2)}, u32[]{:S(2)}) async-start(bf16[8,2,2,128,512]{4,3,2,1,0:T(8,128)(2,1)} %get-tuple-element.89), calls=%async_computation.5 | async-start | bytes 8388608 | tf_op jit(solution)/shard_map/all_to_all | solution.py:905
  182.4 141.6 %reduce-scatter.2.cloned.1.call-start = ((), (), s32[]{:S(2)}) async-start(), calls=%async_computation.10 | async-start | bytes 5242880 | tf_op jit(solution)/shard_map/reduce_scatter | solution.py:1089
  194.3 37.2 %copy-start.13 = (f32[128,512]{1,0:T(8,128)}, f32[128,512]{1,0:T(8,128)S(1)}, u32[]{:S(2)}) copy-start(f32[128,512]{1,0:T(8,128)S(1)} %broadcast_dynamic-update-slice_fusion.extra_ref) | copy-start | bytes 786436
  231.5 54.1 %all-to-all-start.4 = ((bf16[8,2,2,128,512]{4,3,2,1,0:T(8,128)(2,1)}), bf16[8,2,2,128,512]{4,3,2,1,0:T(8,128)(2,1)}, u32[]{:S(2)}, u32[]{:S(2)}) async-start(bf16[8,2,2,128,512]{4,3,2,1,0:T(8,128)(2,1)} %get-tuple-element.79), calls=%async_computation.4 | async-start | bytes 8388608 | tf_op jit(solution)/shard_map/all_to_all | solution.py:905
  304.3 38.8 %copy-start.2 = (bf16[8,197,512]{2,1,0:T(8,128)(2,1)S(1)}, bf16[8,197,512]{2,1,0:T(8,128)(2,1)}, u32[]{:S(2)}) copy-start(bf16[8,197,512]{2,1,0:T(8,128)(2,1)} %get-tuple-element.150) | copy-start | bytes 4841476
  304.3 45.4 %all-to-all-start.7 = ((bf16[16,16,2176]{2,1,0:T(8,128)(2,1)}), bf16[16,16,2176]{2,1,0:T(8,128)(2,1)S(1)}, u32[]{:S(2)}, u32[]{:S(2)}) async-start(bf16[16,16,2176]{2,1,0:T(8,128)(2,1)} %reduce_sum.22), calls=%async_computation.7 | async-start | bytes 2228224 | tf_op jit(solution)/shard_map/all_to_all | solution.py:1160
  324.0 20.8 %copy-start.3 = (bf16[8,197,512]{2,1,0:T(8,128)(2,1)S(1)}, bf16[8,197,512]{2,1,0:T(8,128)(2,1)}, u32[]{:S(2)}) copy-start(bf16[8,197,512]{2,1,0:T(8,128)(2,1)} %get-tuple-element.151) | copy-start | bytes 4841476
  326.2 8.5 %collective-permute-start.4 = (bf16[128,512]{1,0:T(8,128)(2,1)S(1)}, bf16[128,512]{1,0:T(8,128)(2,1)S(1)}, u32[]{:S(2)}, u32[]{:S(2)}) collective-permute-start(bf16[128,512]{1,0:T(8,128)(2,1)S(1)} %get-tuple-element.177), channel_id=1, source_target_pairs={{0,7},{1,6},{2,5},{3,4},{4,3},{5,2},{6,1},{7,0},{8,15},{9,14},{10,... | collective-permute-start | bytes 393224 | tf_op jit(solution)/shard_map/ppermute | solution.py:1098
  328.2 15.0 %collective-permute-start.5 = (bf16[128,512]{1,0:T(8,128)(2,1)S(1)}, bf16[128,512]{1,0:T(8,128)(2,1)S(1)}, u32[]{:S(2)}, u32[]{:S(2)}) collective-permute-start(bf16[128,512]{1,0:T(8,128)(2,1)S(1)} %get-tuple-element.176), channel_id=1, source_target_pairs={{0,6},{1,7},{2,4},{3,5},{4,2},{5,3},{6,0},{7,1},{8,14},{9,15},{10,... | collective-permute-start | bytes 393224 | tf_op jit(solution)/shard_map/ppermute | solution.py:1098
  329.0 20.7 %collective-permute-start.6 = (bf16[128,512]{1,0:T(8,128)(2,1)}, bf16[128,512]{1,0:T(8,128)(2,1)S(1)}, u32[]{:S(2)}, u32[]{:S(2)}) collective-permute-start(bf16[128,512]{1,0:T(8,128)(2,1)} %get-tuple-element.175), channel_id=1, source_target_pairs={{0,5},{1,4},{2,7},{3,6},{4,1},{5,0},{6,3},{7,2},{8,13},{9,12},{10,... | collective-permute-start | bytes 393224 | tf_op jit(solution)/shard_map/ppermute | solution.py:1098
  330.5 19.3 %collective-permute-start.7 = (bf16[128,512]{1,0:T(8,128)(2,1)}, bf16[128,512]{1,0:T(8,128)(2,1)S(1)}, u32[]{:S(2)}, u32[]{:S(2)}) collective-permute-start(bf16[128,512]{1,0:T(8,128)(2,1)} %get-tuple-element.174), channel_id=1, source_target_pairs={{0,4},{1,5},{2,6},{3,7},{4,0},{5,1},{6,2},{7,3},{8,12},{9,13},{10,... | collective-permute-start | bytes 393224 | tf_op jit(solution)/shard_map/ppermute | solution.py:1098
  330.7 19.0 %collective-permute-start.8 = (bf16[128,512]{1,0:T(8,128)(2,1)}, bf16[128,512]{1,0:T(8,128)(2,1)}, u32[]{:S(2)}, u32[]{:S(2)}) collective-permute-start(bf16[128,512]{1,0:T(8,128)(2,1)} %get-tuple-element.173), channel_id=1, source_target_pairs={{0,3},{1,2},{2,1},{3,0},{4,7},{5,6},{6,5},{7,4},{8,11},{9,10},{10,... | collective-permute-start | bytes 393224 | tf_op jit(solution)/shard_map/ppermute | solution.py:1098
  334.7 11.7 %copy-start.7 = (bf16[128,512]{1,0:T(8,128)(2,1)}, bf16[128,512]{1,0:T(8,128)(2,1)S(1)}, u32[]{:S(2)}) copy-start(bf16[128,512]{1,0:T(8,128)(2,1)S(1)} %collective-permute-done.4.refs_0_) | copy-start | bytes 393220
  334.7 17.1 %collective-permute-start.9 = (bf16[128,512]{1,0:T(8,128)(2,1)S(1)}, bf16[128,512]{1,0:T(8,128)(2,1)}, u32[]{:S(2)}, u32[]{:S(2)}) collective-permute-start(bf16[128,512]{1,0:T(8,128)(2,1)S(1)} %get-tuple-element.172), channel_id=1, source_target_pairs={{0,2},{1,3},{2,0},{3,1},{4,6},{5,7},{6,4},{7,5},{8,10},{9,11},{10,... | collective-permute-start | bytes 393224 | tf_op jit(solution)/shard_map/ppermute | solution.py:1098
  343.1 3.4 copy-start.8
  343.1 8.8 %collective-permute-start.10 = (bf16[128,512]{1,0:T(8,128)(2,1)S(1)}, bf16[128,512]{1,0:T(8,128)(2,1)}, u32[]{:S(2)}, u32[]{:S(2)}) collective-permute-start(bf16[128,512]{1,0:T(8,128)(2,1)S(1)} %get-tuple-element.171), channel_id=1, source_target_pairs={{0,1},{1,0},{2,3},{3,2},{4,5},{5,4},{6,7},{7,6},{8,9},{9,8},{10,11... | collective-permute-start | bytes 393224 | tf_op jit(solution)/shard_map/ppermute | solution.py:1098
  349.8 2.1 copy-start
  349.8 2.1 copy-start.9
  (3 other events, 4.7 us)
Sparse Core Ops, SparseCore 0:
  38.9 82.3 all-gather.1
  195.1 96.0 reduce-scatter.1
